TPU v7x, 128 devices: a whole 4x4x4 slice. The times are simulated.
128 devices in a mesh: dp: 8 (over x, core), resp: 16 (over z, y).
Axes of the slice: x: 4, y: 4, z: 4, core: 2. Of those that a mesh axis runs over, the one named last changes fastest.
Arguments:
- queries: bfloat16 [8, 4096, 4096], P('dp', 'resp'), may hold values from -100 to 100
- response_kv: bfloat16 [8, 4096, 1024], P('dp', 'resp'), may hold values from -8 to 8
- cotangent: bfloat16 [8, 4096, 4096], P('dp', 'resp'), may hold values from -6 to 6
- prompt_kv: bfloat16 [8, 16, 128, 1024], P('dp', 'resp'), may hold values from -6 to 6
- resp_lengths: int32 [8, 16, 4], P('dp', 'resp'), may hold values from 1 to 253, as said below
- resp_prompt: int32 [8, 16, 4], P('dp', 'resp'), may hold values from 0 to 3, as said below
- owners: int32 [8, 4], replicated, may hold values from 0 to 127, as said below
Outputs:
- attn_out: bfloat16 [8, 4096, 4096], P('dp', 'resp')
- grad_queries: bfloat16 [8, 4096, 4096], P('dp', 'resp')
- grad_response_kv: bfloat16 [8, 4096, 1024], P('dp', 'resp')
- grad_prompt_kv: float32 [8, 16, 128, 1024], P('dp', 'resp')
Inputs may be any that keep to these rules, and one draw needn't show every extreme that they name: The 32 owners are distinct devices. `resp_prompt`: in each dp row every prompt index names exactly 16 responses. `resp_lengths`: A device's lengths sum to between 128 and 256; in every dp row some device's lengths sum to exactly 256.
All inputs are finite; a program needn't handle non-finite values.
Results may differ from a plain program's by a relative error of at most 0.0055.
Values may be sent and summed in bfloat16 or wider, within the bound.
A program may use at most 128 MiB of HBM per device.

v0:
```python
import jax
import jax.numpy as jnp
from jax import lax
from jax.sharding import PartitionSpec as P

QUERY_PER_KV = 8
HEAD_SIZE = 128


def local_attention(queries, response_kv, cotangent, prompts, lengths, owner_of):
    tok_count = queries.shape[0]
    prompt_count, prompt_len, feature = prompts.shape
    kv_heads = feature // (2 * HEAD_SIZE)
    half_width = kv_heads * HEAD_SIZE
    score_scale = HEAD_SIZE ** (-0.5)
    ends = jnp.cumsum(lengths)
    starts = ends - lengths
    places = jnp.arange(tok_count, dtype=jnp.int32)
    inside = (places[:, None] >= starts[None, :]) & (places[:, None] < ends[None, :])
    live_slot = jnp.any(inside, axis=1)
    resp_index = jnp.sum(
        jnp.where(inside, jnp.arange(lengths.shape[0], dtype=jnp.int32)[None, :], 0), axis=1
    )
    resp_index = jnp.where(live_slot, resp_index, -1)
    prompt_of = jnp.sum(jnp.where(inside, owner_of[None, :], 0), axis=1)
    key_prompt = jnp.arange(prompt_count * prompt_len, dtype=jnp.int32) // prompt_len
    mask_prompt = (key_prompt[None, :] == prompt_of[:, None]) & live_slot[:, None]
    mask_self = (
        (resp_index[None, :] == resp_index[:, None])
        & (places[None, :] <= places[:, None])
        & live_slot[:, None]
    )
    allowed = jnp.concatenate([mask_prompt, mask_self], axis=1)
    live_float = live_slot.astype(jnp.float32)
    masked = jnp.where(live_slot[:, None], cotangent, jnp.zeros_like(cotangent))
    heads_q = queries.reshape(tok_count, kv_heads, QUERY_PER_KV, HEAD_SIZE).transpose(1, 0, 2, 3)
    heads_d = masked.reshape(tok_count, kv_heads, QUERY_PER_KV, HEAD_SIZE).transpose(1, 0, 2, 3)
    keys_all = jnp.concatenate(
        [
            prompts[:, :, :half_width].reshape(prompt_count * prompt_len, kv_heads, HEAD_SIZE),
            response_kv[:, :half_width].reshape(tok_count, kv_heads, HEAD_SIZE),
        ],
        axis=0,
    ).transpose(1, 0, 2)
    values_all = jnp.concatenate(
        [
            prompts[:, :, half_width:].reshape(prompt_count * prompt_len, kv_heads, HEAD_SIZE),
            response_kv[:, half_width:].reshape(tok_count, kv_heads, HEAD_SIZE),
        ],
        axis=0,
    ).transpose(1, 0, 2)

    def one_head(parts):
        head_queries, head_keys, head_values, head_grad = parts
        scores = (
            jnp.einsum("tgd,kd->tgk", head_queries, head_keys, preferred_element_type=jnp.float32)
            * score_scale
        )
        scores = jnp.where(allowed[:, None, :], scores, -1e30)
        row_max = jnp.max(scores, axis=-1, keepdims=True)
        weights_raw = jnp.exp(scores - row_max)
        weights = weights_raw / jnp.sum(weights_raw, axis=-1, keepdims=True)
        weights_low = weights.astype(jnp.bfloat16)
        mixed = jnp.einsum(
            "tgk,kd->tgd", weights_low, head_values, preferred_element_type=jnp.float32
        )
        head_out = (mixed * live_float[:, None, None]).astype(jnp.bfloat16)
        grad_weights = jnp.einsum(
            "tgd,kd->tgk", head_grad, head_values, preferred_element_type=jnp.float32
        )
        row_delta = jnp.sum(weights * grad_weights, axis=-1, keepdims=True)
        grad_scores = (weights * (grad_weights - row_delta)).astype(jnp.bfloat16)
        grad_head_q = (
            jnp.einsum("tgk,kd->tgd", grad_scores, head_keys, preferred_element_type=jnp.float32)
            * score_scale
        ).astype(jnp.bfloat16)
        grad_keys = (
            jnp.einsum("tgk,tgd->kd", grad_scores, head_queries, preferred_element_type=jnp.float32)
            * score_scale
        )
        grad_values = jnp.einsum(
            "tgk,tgd->kd", weights_low, head_grad, preferred_element_type=jnp.float32
        )
        return (head_out, grad_head_q, grad_keys, grad_values)

    out_heads, grad_q_heads, grad_keys, grad_values = lax.map(
        one_head, (heads_q, keys_all, values_all, heads_d)
    )
    attn_out = out_heads.transpose(1, 0, 2, 3).reshape(tok_count, -1)
    grad_queries = grad_q_heads.transpose(1, 0, 2, 3).reshape(tok_count, -1)
    key_total = prompt_count * prompt_len
    grad_keys = grad_keys.transpose(1, 0, 2).reshape(key_total + tok_count, half_width)
    grad_values = grad_values.transpose(1, 0, 2).reshape(key_total + tok_count, half_width)
    grad_response = jnp.concatenate(
        [grad_keys[key_total:], grad_values[key_total:]], axis=1
    ).astype(jnp.bfloat16)
    grad_prompts = jnp.concatenate(
        [grad_keys[:key_total], grad_values[:key_total]], axis=1
    ).reshape(prompt_count, prompt_len, feature)
    return (attn_out, grad_queries, grad_response, grad_prompts)


def local(queries, response_kv, cotangent, prompt_kv, resp_lengths, resp_prompt, owners):
    dp_count = lax.axis_size("dp")
    resp_count = lax.axis_size("resp")
    my_row = lax.axis_index("dp")
    my_column = lax.axis_index("resp")
    my_device = my_row * resp_count + my_column
    own_slot = prompt_kv[0, 0]
    prompt_len, feature = own_slot.shape
    block_rows = prompt_len // resp_count
    prompt_count = owners.shape[1]
    flat_owners = owners.reshape(-1)
    row_owners = lax.dynamic_index_in_dim(owners, my_row, 0, keepdims=False)
    blocks = own_slot.reshape(resp_count, block_rows, feature)
    outgoing = jnp.broadcast_to(blocks[None], (dp_count, resp_count, block_rows, feature))
    outgoing = outgoing.reshape(dp_count * resp_count, block_rows, feature)
    arrived = lax.all_to_all(outgoing, ("dp", "resp"), split_axis=0, concat_axis=0, tiled=True)
    row_blocks = jnp.take(arrived, row_owners, axis=0)
    prompts = lax.all_gather(row_blocks, "resp", axis=1, tiled=True)
    attn_out, grad_queries, grad_response, grad_prompts = local_attention(
        queries[0], response_kv[0], cotangent[0], prompts, resp_lengths[0, 0], resp_prompt[0, 0]
    )
    summed = lax.psum_scatter(grad_prompts, "resp", scatter_dimension=1, tiled=True)
    owns = flat_owners == my_device
    has_prompt = jnp.any(owns)
    own_index = jnp.sum(jnp.where(owns, jnp.arange(flat_owners.shape[0], dtype=jnp.int32), 0))
    own_row = own_index // prompt_count
    outgoing = (
        jnp.zeros((dp_count * resp_count, block_rows, feature), jnp.float32)
        .at[row_owners]
        .set(summed)
    )
    returned = lax.all_to_all(outgoing, ("dp", "resp"), split_axis=0, concat_axis=0, tiled=True)
    returned = returned.reshape(dp_count, resp_count, block_rows, feature)
    gathered = lax.dynamic_index_in_dim(returned, own_row, 0, keepdims=False).reshape(
        prompt_len, feature
    )
    grad_prompt_kv = jnp.where(has_prompt, gathered, jnp.zeros_like(gathered))
    return (attn_out[None], grad_queries[None], grad_response[None], grad_prompt_kv[None, None])


def solution(mesh):
    placed = (
        P("dp", "resp", None),
        P("dp", "resp", None),
        P("dp", "resp", None),
        P("dp", "resp", None, None),
        P("dp", "resp", None),
        P("dp", "resp", None),
        P(),
    )
    return jax.shard_map(
        local,
        mesh=mesh,
        in_specs=placed,
        out_specs=(
            P("dp", "resp", None),
            P("dp", "resp", None),
            P("dp", "resp", None),
            P("dp", "resp", None, None),
        ),
        check_vma=False,
    )
```

profile of v0, /device:TPU:1, one launch (start us, length us, event | category | flops | bytes accessed | tf_op | source)
XLA Modules:
  0.0 335.8 jit_solution(7917132216311308962)
XLA Ops:
  7.2 2.5 broadcast_in_dim.117
  9.7 11.5 %all-to-all-start = ((bf16[128,8,1024]{2,1,0:T(8,128)(2,1)}), bf16[128,8,1024]{2,1,0:T(8,128)(2,1)S(1)}, u32[]{:S(2)}, u32[]{:S(2)}) async-start(bf16[128,8,1024]{2,1,0:T(8,128)(2,1)} %bitcast.19), calls=%async_computation | async-start | bytes 4194304 | tf_op jit(solution)/shard_map/all_to_all | solution.py:118
  22.0 28.4 %all-to-all-done = bf16[128,8,1024]{2,1,0:T(8,128)(2,1)S(1)} async-done(((bf16[128,8,1024]{2,1,0:T(8,128)(2,1)}), bf16[128,8,1024]{2,1,0:T(8,128)(2,1)S(1)}, u32[]{:S(2)}, u32[]{:S(2)}) %all-to-all-start) | async-done | bytes 2097184 | tf_op jit(solution)/shard_map/all_to_all | solution.py:118
  52.7 3.3 copy.40
  56.1 4.1 %copy.36 = bf16[1,256,4096]{1,2,0:T(8,128)(2,1)} copy(bf16[1,256,4096]{2,1,0:T(8,128)(2,1)} %param.9) | data formatting | bytes 4194304 | tf_op args[0]
  62.8 27.4 %all-gather.2.cloned.1.call-done = bf16[4,128,1024]{2,1,0:T(8,128)(2,1)} async-done(((bf16[4,8,1024]{2,1,0:T(8,128)(2,1)}), bf16[4,128,1024]{2,1,0:T(8,128)(2,1)}) %all-gather.2.cloned.1.call-update) | async-done | bytes 1048592 | tf_op jit(solution)/shard_map/all_gather | solution.py:120
  94.7 87.0 %while.16 = (s32[]{:T(128)}, bf16[4,256,8,128]{3,1,2,0:T(8,128)(2,1)}, bf16[4,256,8,128]{3,1,2,0:T(8,128)(2,1)}, f32[4,768,128]{2,1,0:T(8,128)}, f32[4,768,128]{...) while((s32[]{:T(128)}, ...), condition=%wide.region_8.9_spmd, body=%wide.region_4.8_spmd.sunk | while | flops 2440657664 | bytes 77331624 | solution.py:86
  94.7 6.0 %fusion.125 = (f32[256,8]{0,1:T(8,128)S(1)}, f32[256,8,768]{2,0,1:T(8,128)}) fusion(pred[256,768]{1,0:T(8,128)(4,1)} %get-tuple-element.228, bf16[4,256,8,128]{1,3,2,0:T(8,128)(2,1)S(1)} %get-tuple-element.229, s32[]{:T(128)} %get-tuple-element.211, bf16[4,768,128]{2,1,0:T(8,128)(2,1)} %get-tuple-element.230), kind=kOutput, calls=%fused_computation.100.clone.1 | convolution fusion | flops 408945408 | bytes 7218176 | tf_op jit(solution)/shard_map/while/body/eval_jaxpr/sub | solution.py:61
  100.7 4.6 %multiply_reduce_fusion.2 = (f32[256,8]{0,1:T(8,128)S(1)}, f32[256,8,768]{2,0,1:T(8,128)S(1)}) fusion(f32[256,8,768]{2,0,1:T(8,128)} %get-tuple-element.195, f32[256,8]{0,1:T(8,128)S(1)} %get-tuple-element.196, bf16[4,768,128]{2,1,0:T(8,128)(2,1)S(1)} %get-tuple-element.231, s32[]{:T(128)} %get-tuple-element.211, ...), kind=kOutput, calls=%fused_computation.4.clone.1 | convolution fusion | flops 407369728 | bytes 13321216 | tf_op jit(solution)/shard_map/while/body/eval_jaxpr/tgd,kd->tgk/dot_general | solution.py:68
  106.7 2.8 fusion.127
  111.2 3.3 fusion.129
  116.4 6.1 %fusion.125 = (f32[256,8]{0,1:T(8,128)S(1)}, f32[256,8,768]{2,0,1:T(8,128)}) fusion(pred[256,768]{1,0:T(8,128)(4,1)} %get-tuple-element.228, bf16[4,256,8,128]{1,3,2,0:T(8,128)(2,1)S(1)} %get-tuple-element.229, s32[]{:T(128)} %get-tuple-element.211, bf16[4,768,128]{2,1,0:T(8,128)(2,1)} %get-tuple-element.230), kind=kOutput, calls=%fused_computation.100.clone.1 | convolution fusion | flops 408945408 | bytes 7218176 | tf_op jit(solution)/shard_map/while/body/eval_jaxpr/sub | solution.py:61
  122.5 4.6 %multiply_reduce_fusion.2 = (f32[256,8]{0,1:T(8,128)S(1)}, f32[256,8,768]{2,0,1:T(8,128)S(1)}) fusion(f32[256,8,768]{2,0,1:T(8,128)} %get-tuple-element.195, f32[256,8]{0,1:T(8,128)S(1)} %get-tuple-element.196, bf16[4,768,128]{2,1,0:T(8,128)(2,1)S(1)} %get-tuple-element.231, s32[]{:T(128)} %get-tuple-element.211, ...), kind=kOutput, calls=%fused_computation.4.clone.1 | convolution fusion | flops 407369728 | bytes 13321216 | tf_op jit(solution)/shard_map/while/body/eval_jaxpr/tgd,kd->tgk/dot_general | solution.py:68
  128.4 2.8 fusion.127
  133.0 3.3 fusion.129
  138.2 6.0 %fusion.125 = (f32[256,8]{0,1:T(8,128)S(1)}, f32[256,8,768]{2,0,1:T(8,128)}) fusion(pred[256,768]{1,0:T(8,128)(4,1)} %get-tuple-element.228, bf16[4,256,8,128]{1,3,2,0:T(8,128)(2,1)S(1)} %get-tuple-element.229, s32[]{:T(128)} %get-tuple-element.211, bf16[4,768,128]{2,1,0:T(8,128)(2,1)} %get-tuple-element.230), kind=kOutput, calls=%fused_computation.100.clone.1 | convolution fusion | flops 408945408 | bytes 7218176 | tf_op jit(solution)/shard_map/while/body/eval_jaxpr/sub | solution.py:61
  144.2 4.6 %multiply_reduce_fusion.2 = (f32[256,8]{0,1:T(8,128)S(1)}, f32[256,8,768]{2,0,1:T(8,128)S(1)}) fusion(f32[256,8,768]{2,0,1:T(8,128)} %get-tuple-element.195, f32[256,8]{0,1:T(8,128)S(1)} %get-tuple-element.196, bf16[4,768,128]{2,1,0:T(8,128)(2,1)S(1)} %get-tuple-element.231, s32[]{:T(128)} %get-tuple-element.211, ...), kind=kOutput, calls=%fused_computation.4.clone.1 | convolution fusion | flops 407369728 | bytes 13321216 | tf_op jit(solution)/shard_map/while/body/eval_jaxpr/tgd,kd->tgk/dot_general | solution.py:68
  150.2 2.7 fusion.127
  154.7 3.3 fusion.129
  159.9 6.1 %fusion.125 = (f32[256,8]{0,1:T(8,128)S(1)}, f32[256,8,768]{2,0,1:T(8,128)}) fusion(pred[256,768]{1,0:T(8,128)(4,1)} %get-tuple-element.228, bf16[4,256,8,128]{1,3,2,0:T(8,128)(2,1)S(1)} %get-tuple-element.229, s32[]{:T(128)} %get-tuple-element.211, bf16[4,768,128]{2,1,0:T(8,128)(2,1)} %get-tuple-element.230), kind=kOutput, calls=%fused_computation.100.clone.1 | convolution fusion | flops 408945408 | bytes 7218176 | tf_op jit(solution)/shard_map/while/body/eval_jaxpr/sub | solution.py:61
  166.0 4.6 %multiply_reduce_fusion.2 = (f32[256,8]{0,1:T(8,128)S(1)}, f32[256,8,768]{2,0,1:T(8,128)S(1)}) fusion(f32[256,8,768]{2,0,1:T(8,128)} %get-tuple-element.195, f32[256,8]{0,1:T(8,128)S(1)} %get-tuple-element.196, bf16[4,768,128]{2,1,0:T(8,128)(2,1)S(1)} %get-tuple-element.231, s32[]{:T(128)} %get-tuple-element.211, ...), kind=kOutput, calls=%fused_computation.4.clone.1 | convolution fusion | flops 407369728 | bytes 13321216 | tf_op jit(solution)/shard_map/while/body/eval_jaxpr/tgd,kd->tgk/dot_general | solution.py:68
  171.9 2.7 fusion.127
  176.4 3.3 fusion.129
  188.0 73.8 %reduce-scatter.2.cloned.1.call-done = f32[4,8,1024]{2,1,0:T(8,128)} async-done(((f32[4,128,1024]{2,1,0:T(8,128)}), f32[4,8,1024]{2,1,0:T(8,128)}) %reduce-scatter.2.cloned.1.call-update) | async-done | bytes 131088 | tf_op jit(solution)/shard_map/reduce_scatter | solution.py:124
  261.8 2.5 broadcast_in_dim.121
  266.3 9.5 %all-to-all-start.1 = ((f32[128,8,1024]{2,1,0:T(8,128)}), f32[128,8,1024]{2,1,0:T(8,128)}, u32[]{:S(2)}, u32[]{:S(2)}) async-start(f32[128,8,1024]{2,1,0:T(8,128)} %scatter_fusion), calls=%async_computation.2 | async-start | bytes 8388608 | tf_op jit(solution)/shard_map/all_to_all | solution.py:134
  282.6 2.9 copy.45
  285.5 2.3 broadcast_in_dim_reshape.6
  287.8 2.9 copy.46
  290.7 2.3 broadcast_in_dim_reshape.7
  293.9 32.6 %all-to-all-done.1 = f32[128,8,1024]{2,1,0:T(8,128)} async-done(((f32[128,8,1024]{2,1,0:T(8,128)}), f32[128,8,1024]{2,1,0:T(8,128)}, u32[]{:S(2)}, u32[]{:S(2)}) %all-to-all-start.1) | async-done | bytes 4194336 | tf_op jit(solution)/shard_map/all_to_all | solution.py:134
  326.5 2.5 select_bitcast_fusion.1
  (103 shorter events, 43.6 us)
Async XLA Ops:
  9.7 11.6 %copy-start.3 = (s32[8,4]{0,1:T(4,128)S(1)}, s32[8,4]{0,1:T(4,128)}, u32[]{:S(2)}) copy-start(s32[8,4]{0,1:T(4,128)} %param.15) | copy-start | bytes 388
  9.7 42.1 %copy-start.8 = (s32[1,1,4]{2,1,0:T(1,128)S(1)}, s32[1,1,4]{2,1,0:T(1,128)}, u32[]{:S(2)}) copy-start(s32[1,1,4]{2,1,0:T(1,128)} %param.13) | copy-start | bytes 52
  9.7 42.3 %copy-start.1 = (bf16[1,256,1024]{2,1,0:T(8,128)(2,1)S(1)}, bf16[1,256,1024]{2,1,0:T(8,128)(2,1)}, u32[]{:S(2)}) copy-start(bf16[1,256,1024]{2,1,0:T(8,128)(2,1)} %param.10) | copy-start | bytes 1572868
  9.7 40.8 %all-to-all-start = ((bf16[128,8,1024]{2,1,0:T(8,128)(2,1)}), bf16[128,8,1024]{2,1,0:T(8,128)(2,1)S(1)}, u32[]{:S(2)}, u32[]{:S(2)}) async-start(bf16[128,8,1024]{2,1,0:T(8,128)(2,1)} %bitcast.19), calls=%async_computation | async-start | bytes 4194304 | tf_op jit(solution)/shard_map/all_to_all | solution.py:118
  21.2 68.9 %all-gather.2.cloned.1.call-start = ((), (), s32[]{:S(2)}) async-start(), calls=%async_computation.3 | async-start | bytes 1114112 | tf_op jit(solution)/shard_map/all_gather | solution.py:120
  21.5 0.6 copy-start.5
  51.8 210.1 %reduce-scatter.2.cloned.1.call-start = ((), (), s32[]{:S(2)}) async-start(), calls=%async_computation.4 | async-start | bytes 2228224 | tf_op jit(solution)/shard_map/reduce_scatter | solution.py:124
  56.0 4.1 %copy-start.7 = (s32[1,1,4]{2,1,0:T(1,128)S(1)}, s32[1,1,4]{2,1,0:T(1,128)}, u32[]{:S(2)}) copy-start(s32[1,1,4]{2,1,0:T(1,128)} %param.14) | copy-start | bytes 52
  93.1 1.6 copy-start
  100.7 4.6 %slice-start = ((s8[6291456]{0:T(1024)(128)(4,1)}), s8[4194304]{0:T(1024)(128)(4,1)S(1)}, s32[]{:S(2)}) async-start(s8[6291456]{0:T(1024)(128)(4,1)} %bitcast.141), calls=%async_computation.5 | async-start | bytes 8388608 | tf_op jit(solution)/shard_map/while
  100.7 4.8 %slice-start.1 = ((s8[6291456]{0:T(1024)(128)(4,1)}), s8[2097152]{0:T(1024)(128)(4,1)S(1)}, s32[]{:S(2)}) async-start(s8[6291456]{0:T(1024)(128)(4,1)} %bitcast.141), calls=%async_computation.6 | async-start | bytes 4194304 | tf_op jit(solution)/shard_map/while
  122.5 4.6 %slice-start = ((s8[6291456]{0:T(1024)(128)(4,1)}), s8[4194304]{0:T(1024)(128)(4,1)S(1)}, s32[]{:S(2)}) async-start(s8[6291456]{0:T(1024)(128)(4,1)} %bitcast.141), calls=%async_computation.5 | async-start | bytes 8388608 | tf_op jit(solution)/shard_map/while
  122.5 4.8 %slice-start.1 = ((s8[6291456]{0:T(1024)(128)(4,1)}), s8[2097152]{0:T(1024)(128)(4,1)S(1)}, s32[]{:S(2)}) async-start(s8[6291456]{0:T(1024)(128)(4,1)} %bitcast.141), calls=%async_computation.6 | async-start | bytes 4194304 | tf_op jit(solution)/shard_map/while
  144.2 4.6 %slice-start = ((s8[6291456]{0:T(1024)(128)(4,1)}), s8[4194304]{0:T(1024)(128)(4,1)S(1)}, s32[]{:S(2)}) async-start(s8[6291456]{0:T(1024)(128)(4,1)} %bitcast.141), calls=%async_computation.5 | async-start | bytes 8388608 | tf_op jit(solution)/shard_map/while
  144.2 4.8 %slice-start.1 = ((s8[6291456]{0:T(1024)(128)(4,1)}), s8[2097152]{0:T(1024)(128)(4,1)S(1)}, s32[]{:S(2)}) async-start(s8[6291456]{0:T(1024)(128)(4,1)} %bitcast.141), calls=%async_computation.6 | async-start | bytes 4194304 | tf_op jit(solution)/shard_map/while
  166.0 4.6 %slice-start = ((s8[6291456]{0:T(1024)(128)(4,1)}), s8[4194304]{0:T(1024)(128)(4,1)S(1)}, s32[]{:S(2)}) async-start(s8[6291456]{0:T(1024)(128)(4,1)} %bitcast.141), calls=%async_computation.5 | async-start | bytes 8388608 | tf_op jit(solution)/shard_map/while
  166.0 4.8 %slice-start.1 = ((s8[6291456]{0:T(1024)(128)(4,1)}), s8[2097152]{0:T(1024)(128)(4,1)S(1)}, s32[]{:S(2)}) async-start(s8[6291456]{0:T(1024)(128)(4,1)} %bitcast.141), calls=%async_computation.6 | async-start | bytes 4194304 | tf_op jit(solution)/shard_map/while
  188.0 76.3 %copy-start.6 = (s32[4]{0:T(128)S(1)}, s32[4]{0:T(128)}, u32[]{:S(2)}) copy-start(s32[4]{0:T(128)} %copy-done.5) | copy-start | bytes 52
  261.8 2.5 copy-start.2
  266.3 9.5 %copy-start.4 = (s32[8,4]{0,1:T(4,128)S(1)}, s32[8,4]{0,1:T(4,128)}, u32[]{:S(2)}) copy-start(s32[8,4]{0,1:T(4,128)} %param.15) | copy-start | bytes 388
  266.3 60.2 %all-to-all-start.1 = ((f32[128,8,1024]{2,1,0:T(8,128)}), f32[128,8,1024]{2,1,0:T(8,128)}, u32[]{:S(2)}, u32[]{:S(2)}) async-start(f32[128,8,1024]{2,1,0:T(8,128)} %scatter_fusion), calls=%async_computation.2 | async-start | bytes 8388608 | tf_op jit(solution)/shard_map/all_to_all | solution.py:134
Sparse Core Ops, SparseCore 0:
  51.9 38.2 all-gather.1
  188.1 73.6 reduce-scatter.1
where the time goes:
time: 338 us; the launch traced here: 336 us
  waiting for transfers between devices  162 us (48%)
  matrix products  81.4 us (24%)
  local copies, waits for them, and re-layouts  38.8 us (11%)
  starting transfers between devices  21.1 us (6%)
  between operations  17 us (5%)
  other arithmetic  15.3 us (5%)
    reduce_scatter x1, waiting for transfers between devices, local(): lax.psum_scatter(grad_prompts, 'resp', scatter_dimension=1, tiled=True)  73.8 us
    all_to_all x2, waiting for transfers between devices, local(): lax.all_to_all(outgoing, ('dp', 'resp'), split_axis=0, concat_axis=0, til...  61 us
    all_gather x1, waiting for transfers between devices, local(): prompts = lax.all_gather(row_blocks, 'resp', axis=1, tiled=True)  27.4 us
    sub x4, matrix products, one_head(): weights_raw = jnp.exp(scores - row_max)  24.2 us
    all_to_all x2, starting transfers between devices, local(): lax.all_to_all(outgoing, ('dp', 'resp'), split_axis=0, concat_axis=0, til...  21 us
    dot_general x4, matrix products, one_head(): jnp.einsum('tgd,kd->tgk', head_grad, head_values, preferred_element_type=...  18.3 us
    dot_general x4, matrix products, one_head(): jnp.einsum('tgk,tgd->kd', weights_low, head_grad, preferred_element_type=...  13.1 us
    dot_general x4, matrix products, one_head(): jnp.einsum('tgk,kd->tgd', grad_scores, head_keys, preferred_element_type=...  11 us
  transfers between devices with their start and end apart: 4, of which 4 were waited for; matrix products, arithmetic and copies ran while one was open for 8% of the time, Pallas kernels for 0%

commit v1 on v0

v1 whole, which is shorter than its diff:
```python
import jax
import jax.numpy as jnp
from jax import lax
from jax.experimental import pallas as pl
from jax.experimental.pallas import tpu as pltpu
from jax.sharding import PartitionSpec as P

F32 = jnp.float32
BF16 = jnp.bfloat16
HEAD = 128
QPK = 8
KVH = 4
TOK = 256
LP = 128
NP = 4
HALF = KVH * HEAD
NEG = -1e30
SCALE = HEAD ** -0.5
EXP2_SCALE = SCALE * 1.4426950408889634

NN = (((1,), (0,)), ((), ()))
NT = (((1,), (1,)), ((), ()))


def dot(a, b, dims):
    return lax.dot_general(a, b, dims, preferred_element_type=F32)


def cols(index, width=HEAD):
    return pl.ds(pl.multiple_of(index * width, width), width)


def build_masks(len_ref, prm_ref, bias, qmask, lmask):
    def slot_ids(place):
        resp = jnp.full(place.shape, -1, jnp.int32)
        prompt = jnp.full(place.shape, -1, jnp.int32)
        start = jnp.int32(0)
        for i in range(4):
            end = start + len_ref[0, i]
            inside = (place >= start) & (place < end)
            resp = jnp.where(inside, i, resp)
            prompt = jnp.where(inside, prm_ref[0, i], prompt)
            start = end
        return resp, prompt

    keys = lax.broadcasted_iota(jnp.int32, (TOK, TOK), 0)
    slots = lax.broadcasted_iota(jnp.int32, (TOK, TOK), 1)
    key_resp, _ = slot_ids(keys)
    slot_resp, _ = slot_ids(slots)
    allowed = (key_resp == slot_resp) & (keys <= slots) & (slot_resp >= 0)
    bias[...] = jnp.where(allowed, 0.0, NEG)
    _, by_row = slot_ids(lax.broadcasted_iota(jnp.int32, (TOK, HEAD), 0))
    _, by_lane = slot_ids(lax.broadcasted_iota(jnp.int32, (LP, TOK), 1))
    for j in range(NP):
        qmask[j] = jnp.where(by_row == j, 1.0, 0.0).astype(BF16)
        lmask[j] = jnp.where(by_lane == j, 1.0, 0.0).astype(BF16)


def self_scores(n, q_ref, do_ref, kv_ref, bias, e_self, dp_self, stat):
    h = n // QPK
    keys = kv_ref[:, cols(h)]
    values = kv_ref[:, cols(h + KVH)]
    raw = dot(keys, q_ref[:, cols(n)], NT) + bias[...]
    top = jnp.max(raw, axis=0, keepdims=True)
    e = jnp.exp2((raw - top) * EXP2_SCALE)
    dp = dot(values, do_ref[:, cols(n)], NT)
    e_self[n] = e
    dp_self[n] = dp
    stat[n, 0:1, :] = top
    stat[n, 1:2, :] = jnp.sum(e, axis=0, keepdims=True)
    stat[n, 2:3, :] = jnp.sum(e * dp, axis=0, keepdims=True)


def prompt_scores(n, q_ref, do_ref, qmask, kcat, vcat, w_pr, ds_pr, stat, dk_acc, dv_acc):
    h = n // QPK
    q = q_ref[:, cols(n)]
    do = do_ref[:, cols(n)]
    qe = jnp.concatenate([q * qmask[j] for j in range(NP)], axis=1)
    de = jnp.concatenate([do * qmask[j] for j in range(NP)], axis=1)
    raw = dot(kcat[h], qe, NT)
    dp = dot(vcat[h], de, NT)
    top_self = stat[n, 0:1, :]
    top = jnp.maximum(jnp.max(raw, axis=0, keepdims=True), top_self)
    e = jnp.exp2((raw - top) * EXP2_SCALE)
    shrink = jnp.exp2((top_self - top) * EXP2_SCALE)
    total = jnp.sum(e, axis=0, keepdims=True) + shrink * stat[n, 1:2, :]
    inverse = 1.0 / total
    delta = (jnp.sum(e * dp, axis=0, keepdims=True) + shrink * stat[n, 2:3, :]) * inverse
    w = e * inverse
    ds = (w * (dp - delta)).astype(BF16)
    w = w.astype(BF16)
    stat[n, 3:4, :] = shrink * inverse
    stat[n, 4:5, :] = delta
    w_pr[n] = w
    ds_pr[n] = ds
    return dot(ds, qe, NN), dot(w, de, NN)


def finish(n, q_ref, do_ref, lmask, kt, vt, e_self, dp_self, w_pr, ds_pr, stat, out_ref, dq_ref):
    h = n // QPK
    w = e_self[n] * stat[n, 3:4, :]
    ds = (w * (dp_self[n] - stat[n, 4:5, :])).astype(BF16)
    w = w.astype(BF16)
    w_all = jnp.concatenate([w_pr[n] * lmask[j] for j in range(NP)] + [w], axis=0)
    ds_all = jnp.concatenate([ds_pr[n] * lmask[j] for j in range(NP)] + [ds], axis=0)
    out = dot(vt[h], w_all, NN).astype(BF16)
    dq = (dot(kt[h], ds_all, NN) * SCALE).astype(BF16)
    out_ref[:, cols(n)] = out.T
    dq_ref[:, cols(n)] = dq.T
    return dot(ds, q_ref[:, cols(n)], NN), dot(w, do_ref[:, cols(n)], NN)


def prompt_tables(pr_ref, kcat, vcat):
    for h in range(KVH):
        for j in range(NP):
            kcat[h, :, j * HEAD:(j + 1) * HEAD] = pr_ref[j, :, h * HEAD:(h + 1) * HEAD]
            vcat[h, :, j * HEAD:(j + 1) * HEAD] = pr_ref[j, :, HALF + h * HEAD:HALF + (h + 1) * HEAD]


def transposed_tables(pr_ref, kv_ref, kt, vt):
    for h in range(KVH):
        for j in range(NP):
            kt[h, :, j * LP:(j + 1) * LP] = pr_ref[j, :, h * HEAD:(h + 1) * HEAD].T
            vt[h, :, j * LP:(j + 1) * LP] = pr_ref[j, :, HALF + h * HEAD:HALF + (h + 1) * HEAD].T
        kt[h, :, NP * LP:] = kv_ref[:, h * HEAD:(h + 1) * HEAD].T
        vt[h, :, NP * LP:] = kv_ref[:, HALF + h * HEAD:HALF + (h + 1) * HEAD].T


N_DP = 8
N_RESP = 16
CH = 16
HEADS = KVH * QPK
STEP = 2
SELF_CUTS = (0, 10, 20, 32)
FINISH_CUTS = (0, 12, 22, 32)
MESH = pl.DeviceIdType.MESH


def kernel(
    q_hbm, do_hbm, kv_hbm, slot_ref, len_ref, prm_ref, own_ref,
    out_hbm, dq_hbm, gr_hbm, gp_out,
    q_ref, do_ref, kv_ref, out_ref, dq_ref, gr_ref,
    bias, qmask, lmask, e_self, dp_self, stat, kcat, vcat, kt, vt, w_pr, ds_pr, dk_acc, dv_acc, dks, dvs,
    buf1, send2, recv2, mine, pall, gp, gland, gmine, gland2, send3, fin, inv,
    in_sem, out_sem, s1, r1, s2, r2, s3, r3, s4, r4, s5, r5, s6, r6,
):
    a = lax.axis_index("dp")
    c = lax.axis_index("resp")

    loads = [
        pltpu.make_async_copy(src, dst, in_sem.at[i])
        for i, (src, dst) in enumerate(((kv_hbm, kv_ref), (q_hbm, q_ref), (do_hbm, do_ref)))
    ]
    for load in loads:
        load.start()

    def col_peer(d):
        return lax.rem(c + d, N_RESP)

    def row_peer(d):
        return lax.rem(a + d, N_DP)

    def chunk(index):
        half = index // 8
        block = lax.rem(index, 8)
        return pl.ds(pl.multiple_of(block * CH, CH), CH), half

    def chunk_cols(index):
        rows, half = chunk(index)
        return rows, pl.ds(pl.multiple_of(half * HALF, HALF), HALF)

    def send(src, dst, ssem, rsem, device):
        return pltpu.make_async_remote_copy(
            src_ref=src, dst_ref=dst, send_sem=ssem, recv_sem=rsem, device_id=device, device_id_type=MESH
        )

    barrier = pltpu.get_barrier_semaphore()
    for d in range(1, N_RESP):
        pl.semaphore_signal(barrier, inc=1, device_id=(a, col_peer(d)), device_id_type=MESH)
    for d in range(1, N_DP):
        pl.semaphore_signal(barrier, inc=1, device_id=(row_peer(d), c), device_id_type=MESH)
    build_masks(len_ref, prm_ref, bias, qmask, lmask)
    pl.semaphore_wait(barrier, N_RESP - 1 + N_DP - 1)

    sent = []
    first = []
    for d in range(1, N_RESP):
        to = col_peer(d)
        rows, lanes = chunk_cols(to)
        copy = send(slot_ref.at[rows, lanes], buf1.at[d], s1.at[d - 1], r1.at[d - 1], (a, to))
        copy.start()
        first.append(copy)
    rows, lanes = chunk_cols(c)
    buf1[0] = slot_ref[rows, lanes]

    @pl.loop(0, N_RESP)
    def _(d):
        device = a * N_RESP + lax.rem(c + d, N_RESP)
        found = jnp.int32(-1)
        for k in range(N_DP * NP):
            found = jnp.where(own_ref[k // NP, k % NP] == device, k, found)
        inv[d] = found

    for load in loads:
        load.wait()

    def self_part(lo, hi):
        @pl.loop(lo // STEP, hi // STEP)
        def _(i):
            for u in range(STEP):
                self_scores(i * STEP + u, q_ref, do_ref, kv_ref, bias, e_self, dp_self, stat)

    self_part(SELF_CUTS[0], SELF_CUTS[1])

    for copy in first:
        copy.wait_recv()
    second = []
    for d in range(N_DP):
        to = row_peer(d)
        for j in range(NP):
            column = jnp.bitwise_and(own_ref[to, j], N_RESP - 1)
            piece = buf1[lax.rem(c + N_RESP - column, N_RESP)]
            if d == 0:
                recv2[0, j] = piece
            else:
                send2[d - 1, j] = piece
        if d:
            copy = send(send2.at[d - 1], recv2.at[d], s2.at[d - 1], r2.at[d - 1], (to, c))
            copy.start()
            second.append(copy)

    self_part(SELF_CUTS[1], SELF_CUTS[2])

    for copy in second:
        copy.wait_recv()
    rows, lanes = chunk_cols(c)
    for j in range(NP):
        owner_row = jnp.right_shift(own_ref[a, j], 4)
        piece = recv2[lax.rem(a + N_DP - owner_row, N_DP), j]
        mine[j] = piece
        pall[j, rows, lanes] = piece
    third = []
    for d in range(1, N_RESP):
        copy = send(mine, pall.at[:, rows, lanes], s3.at[d - 1], r3.at[d - 1], (a, col_peer(d)))
        copy.start()
        third.append(copy)

    self_part(SELF_CUTS[2], SELF_CUTS[3])

    for d in range(1, N_RESP):
        rows_in, lanes_in = chunk_cols(lax.rem(c + N_RESP - d, N_RESP))
        send(mine, pall.at[:, rows_in, lanes_in], s3.at[d - 1], r3.at[d - 1], (a, col_peer(d))).wait_recv()

    prompt_tables(pall, kcat, vcat)
    fourth = []
    for h in range(KVH):
        dk_acc[h] = jnp.zeros((LP, NP * HEAD), F32)
        dv_acc[h] = jnp.zeros((LP, NP * HEAD), F32)

        @pl.loop(0, QPK // STEP)
        def _(i):
            parts = [
                prompt_scores(h * QPK + i * STEP + u, q_ref, do_ref, qmask, kcat, vcat, w_pr, ds_pr, stat, dk_acc, dv_acc)
                for u in range(STEP)
            ]
            dk_acc[h] += sum(p[0] for p in parts)
            dv_acc[h] += sum(p[1] for p in parts)

        for j in range(NP):
            gp[h, 0, j] = (dk_acc[h, :, j * HEAD:(j + 1) * HEAD] * SCALE).astype(BF16)
            gp[h, 1, j] = dv_acc[h, :, j * HEAD:(j + 1) * HEAD].astype(BF16)
        for d in range(1, N_RESP):
            to = col_peer(d)
            rows_to, half_to = chunk(to)
            copy = send(
                gp.at[h, half_to, :, rows_to, :], gland.at[d - 1, h], s4.at[h, d - 1], r4.at[h, d - 1], (a, to)
            )
            copy.start()
            fourth.append(copy)

    transposed_tables(pall, kv_ref, kt, vt)
    dks[...] = jnp.zeros_like(dks)
    dvs[...] = jnp.zeros_like(dvs)

    def finish_part(lo, hi):
        @pl.loop(lo // STEP, hi // STEP)
        def _(i):
            parts = [
                finish(i * STEP + u, q_ref, do_ref, lmask, kt, vt, e_self, dp_self, w_pr, ds_pr, stat, out_ref, dq_ref)
                for u in range(STEP)
            ]
            h = i * STEP // QPK
            dks[h] += sum(p[0] for p in parts)
            dvs[h] += sum(p[1] for p in parts)

    finish_part(FINISH_CUTS[0], FINISH_CUTS[1])

    for copy in fourth:
        copy.wait_recv()
    rows, half = chunk(c)
    for h in range(KVH):
        for j in range(NP):
            total = gp[h, half, j, rows, :].astype(F32)
            for d in range(1, N_RESP):
                total += gland[d - 1, h, j].astype(F32)
            gmine[h, j] = total.astype(BF16)
    gland2[0] = gmine[...]
    fifth = []
    for d in range(1, N_DP):
        copy = send(gmine, gland2.at[d], s5.at[d - 1], r5.at[d - 1], (row_peer(d), c))
        copy.start()
        fifth.append(copy)

    finish_part(FINISH_CUTS[1], FINISH_CUTS[2])

    for copy in fifth:
        copy.wait_recv()
    sixth = []
    for d in range(N_RESP):
        index = inv[d]
        has = index >= 0
        at = jnp.maximum(index, 0)
        row = jnp.right_shift(at, 2)
        j = jnp.bitwise_and(at, 3)
        for h in range(KVH):
            piece = gland2[lax.rem(a + N_DP - row, N_DP), h, j].astype(F32)
            piece = jnp.where(has, piece, 0.0).astype(BF16)
            if d == 0:
                fin[0, h] = piece
            else:
                send3[d - 1, h] = piece
        if d:
            copy = send(send3.at[d - 1], fin.at[d], s6.at[d - 1], r6.at[d - 1], (a, col_peer(d)))
            copy.start()
            sixth.append(copy)

    finish_part(FINISH_CUTS[2], FINISH_CUTS[3])

    for h in range(KVH):
        gr_ref[:, h * HEAD:(h + 1) * HEAD] = (dks[h] * SCALE).astype(BF16)
        gr_ref[:, HALF + h * HEAD:HALF + (h + 1) * HEAD] = dvs[h].astype(BF16)
    stores = [
        pltpu.make_async_copy(src, dst, out_sem.at[i])
        for i, (src, dst) in enumerate(((out_ref, out_hbm), (dq_ref, dq_hbm), (gr_ref, gr_hbm)))
    ]
    for store in stores:
        store.start()

    for copy in sixth:
        copy.wait_recv()
    for d in range(N_RESP):
        rows_in, half_in = chunk(lax.rem(c + N_RESP - d, N_RESP))
        for h in range(KVH):
            lanes_in = pl.ds(pl.multiple_of(half_in * HALF + h * HEAD, HEAD), HEAD)
            gp_out[rows_in, lanes_in] = fin[d, h].astype(F32)

    for copy in first + second + third + fourth + fifth + sixth:
        copy.wait_send()
    for store in stores:
        store.wait()


def local(queries, response_kv, cotangent, prompt_kv, resp_lengths, resp_prompt, owners):
    vm = pl.BlockSpec(memory_space=pltpu.VMEM)
    sm = pl.BlockSpec(memory_space=pltpu.SMEM)
    hbm = pl.BlockSpec(memory_space=pl.ANY)
    peers = (N_RESP - 1,)
    row_peers = (N_DP - 1,)
    dma = pltpu.SemaphoreType.DMA
    outs = pl.pallas_call(
        kernel,
        in_specs=[hbm, hbm, hbm, vm, sm, sm, sm],
        out_specs=[hbm, hbm, hbm, vm],
        out_shape=[
            jax.ShapeDtypeStruct((TOK, 4096), BF16),
            jax.ShapeDtypeStruct((TOK, 4096), BF16),
            jax.ShapeDtypeStruct((TOK, 1024), BF16),
            jax.ShapeDtypeStruct((LP, 1024), F32),
        ],
        scratch_shapes=[
            pltpu.VMEM((TOK, 4096), BF16),
            pltpu.VMEM((TOK, 4096), BF16),
            pltpu.VMEM((TOK, 1024), BF16),
            pltpu.VMEM((TOK, 4096), BF16),
            pltpu.VMEM((TOK, 4096), BF16),
            pltpu.VMEM((TOK, 1024), BF16),
            pltpu.VMEM((TOK, TOK), F32),
            pltpu.VMEM((NP, TOK, HEAD), BF16),
            pltpu.VMEM((NP, LP, TOK), BF16),
            pltpu.VMEM((HEADS, TOK, TOK), F32),
            pltpu.VMEM((HEADS, TOK, TOK), F32),
            pltpu.VMEM((HEADS, 8, TOK), F32),
            pltpu.VMEM((KVH, LP, NP * HEAD), BF16),
            pltpu.VMEM((KVH, LP, NP * HEAD), BF16),
            pltpu.VMEM((KVH, HEAD, NP * LP + TOK), BF16),
            pltpu.VMEM((KVH, HEAD, NP * LP + TOK), BF16),
            pltpu.VMEM((HEADS, LP, TOK), BF16),
            pltpu.VMEM((HEADS, LP, TOK), BF16),
            pltpu.VMEM((KVH, LP, NP * HEAD), F32),
            pltpu.VMEM((KVH, LP, NP * HEAD), F32),
            pltpu.VMEM((KVH, TOK, HEAD), F32),
            pltpu.VMEM((KVH, TOK, HEAD), F32),
            pltpu.VMEM((N_RESP, CH, HALF), BF16),
            pltpu.VMEM((N_DP - 1, NP, CH, HALF), BF16),
            pltpu.VMEM((N_DP, NP, CH, HALF), BF16),
            pltpu.VMEM((NP, CH, HALF), BF16),
            pltpu.VMEM((NP, LP, 2 * HALF), BF16),
            pltpu.VMEM((KVH, 2, NP, LP, HEAD), BF16),
            pltpu.VMEM((N_RESP - 1, KVH, NP, CH, HEAD), BF16),
            pltpu.VMEM((KVH, NP, CH, HEAD), BF16),
            pltpu.VMEM((N_DP, KVH, NP, CH, HEAD), BF16),
            pltpu.VMEM((N_RESP - 1, KVH, CH, HEAD), BF16),
            pltpu.VMEM((N_RESP, KVH, CH, HEAD), BF16),
            pltpu.SMEM((N_RESP,), jnp.int32),
            dma((3,)), dma((3,)),
            dma(peers), dma(peers),
            dma(row_peers), dma(row_peers),
            dma(peers), dma(peers),
            dma((KVH,) + peers), dma((KVH,) + peers),
            dma(row_peers), dma(row_peers),
            dma(peers), dma(peers),
        ],
        compiler_params=pltpu.CompilerParams(
            collective_id=0, has_side_effects=True, vmem_limit_bytes=56 * 2 ** 20
        ),
        name="grouped_attention",
    )(
        queries[0], cotangent[0], response_kv[0], prompt_kv[0, 0],
        resp_lengths[0], resp_prompt[0], owners,
    )
    attn_out, grad_queries, grad_response, grad_prompt = outs
    return attn_out[None], grad_queries[None], grad_response[None], grad_prompt[None, None]


def solution(mesh):
    placed = (
        P("dp", "resp", None),
        P("dp", "resp", None),
        P("dp", "resp", None),
        P("dp", "resp", None, None),
        P("dp", "resp", None),
        P("dp", "resp", None),
        P(),
    )
    return jax.shard_map(
        local,
        mesh=mesh,
        in_specs=placed,
        out_specs=(
            P("dp", "resp", None),
            P("dp", "resp", None),
            P("dp", "resp", None),
            P("dp", "resp", None, None),
        ),
        check_vma=False,
    )
```

time: 338 us -> 83.3 us (0.25)
  waiting for transfers between devices: 162 us -> 0 us
  matrix products: 81.4 us -> 0 us
  Pallas kernels: 0 us -> 74.9 us
  local copies, waits for them, and re-layouts: 38.8 us -> 7.59 us
  starting transfers between devices: 21.1 us -> 0 us
  between operations: 17 us -> 0.65 us
  other arithmetic: 15.3 us -> 0 us
    pallas_call x0 -> x1, Pallas kernels: none -> 74.9 us  [local(): pl.pallas_call(kernel, in_specs=[hbm, hbm, hbm, vm, sm, sm, sm], out_spec...]
    reduce_scatter x1 -> x0, waiting for transfers between devices: 73.8 us -> none  [local(): lax.psum_scatter(grad_prompts, 'resp', scatter_dimension=1, tiled=True)]
    all_to_all x2 -> x0, waiting for transfers between devices: 61 us -> none  [local(): lax.all_to_all(outgoing, ('dp', 'resp'), split_axis=0, concat_axis=0, til...]
    dot_general x20 -> x0, matrix products: 57.2 us -> none  [the longest x4 18.3 us: one_head(): jnp.einsum('tgd,kd->tgk', head_grad, head_values, preferred_element_type=...]
    all_gather x1 -> x0, waiting for transfers between devices: 27.4 us -> none  [local(): prompts = lax.all_gather(row_blocks, 'resp', axis=1, tiled=True)]
    sub x4 -> x0, matrix products: 24.2 us -> none  [one_head(): weights_raw = jnp.exp(scores - row_max)]
    all_to_all x2 -> x0, starting transfers between devices: 21 us -> none  [local(): lax.all_to_all(outgoing, ('dp', 'resp'), split_axis=0, concat_axis=0, til...]
    slice x10 -> x0, local copies, waits for them, and re-layouts: 7.87 us -> none  [the longest x2 1.98 us: local_attention(): grad_values[:key_total]]
  transfers between devices with their start and end apart: 4 -> 0, of which waited for: 4 -> 0; matrix products, arithmetic and copies ran while one was open for 8% -> 0% of each run, Pallas kernels for 0% -> 0%
where the time goes in v1:
time: 83.3 us; the launch traced here: 83.2 us
  Pallas kernels  74.9 us (90%)
  local copies, waits for them, and re-layouts  7.59 us (9%)
    pallas_call x1, Pallas kernels, local(): pl.pallas_call(kernel, in_specs=[hbm, hbm, hbm, vm, sm, sm, sm], out_spec...  74.9 us
    unnamed x11, local copies, waits for them, and re-layouts  7.59 us

profile of v1, /device:TPU:1, one launch (start us, length us, event | category | flops | bytes accessed | tf_op | source)
XLA Modules:
  0.0 83.2 jit_solution(7681718548904890379)
XLA Ops:
  0.6 1.3 %copy.11.own_ref = s32[8,4]{1,0:T(8,128)} copy(s32[8,4]{0,1:T(4,128)} %param.13) | data formatting | bytes 256 | tf_op args[6]
  2.0 74.9 %grouped_attention.1 = (bf16[256,4096]{1,0:T(8,128)(2,1)}, bf16[256,4096]{1,0:T(8,128)(2,1)}, bf16[256,1024]{1,0:T(8,128)(2,1)}, f32[128,1024]{1,0:T(8,128)}) custom-call(bf16[256,4096]{1,0:T(8,128)(2,1)} %bitcast.10, bf16[256,4096]{1,0:T(8,128)(2,1)} %bitcast.11, bf16[256,1024]{1,0:T(8,128)(2,1)} %bitcast.14, bf16[128,1024]{1,0:T(8,128)(2,1)} %bitcast.17, ...), custom_call_target="tpu_custom_call" | custom-call | tf_op jit(solution)/shard_map/grouped_attention/pallas_call | solution.py:370
  76.9 0.0 copy-start
  76.9 3.3 %copy.16 = bf16[1,256,4096]{2,1,0:T(8,128)(2,1)} copy(bf16[1,256,4096]{2,1,0:T(8,128)(2,1)} %bitcast.13) | data formatting | bytes 4194304
  80.2 0.0 copy-done
  80.2 0.0 copy-start.2
  80.2 0.0 copy-start.1
  80.2 1.3 %copy.17 = bf16[1,256,4096]{2,1,0:T(8,128)(2,1)} copy(bf16[1,256,4096]{2,1,0:T(8,128)(2,1)S(1)} %bitcast.12) | data formatting | bytes 4194304
  81.5 0.1 copy-done.2
  81.6 0.8 copy.18
  82.4 0.0 copy-done.1
  82.4 0.8 copy.19
Async XLA Ops:
  76.9 3.3 %copy-start = (bf16[256,4096]{1,0:T(8,128)(2,1)S(1)}, bf16[256,4096]{1,0:T(8,128)(2,1)}, u32[]{:S(2)}) copy-start(bf16[256,4096]{1,0:T(8,128)(2,1)} %get-tuple-element.9) | copy-start | bytes 6291460
  80.2 1.4 %copy-start.2 = (bf16[256,1024]{1,0:T(8,128)(2,1)S(1)}, bf16[256,1024]{1,0:T(8,128)(2,1)}, u32[]{:S(2)}) copy-start(bf16[256,1024]{1,0:T(8,128)(2,1)} %get-tuple-element.10) | copy-start | bytes 1572868
  80.2 2.2 %copy-start.1 = (f32[128,1024]{1,0:T(8,128)S(1)}, f32[128,1024]{1,0:T(8,128)}, u32[]{:S(2)}) copy-start(f32[128,1024]{1,0:T(8,128)} %get-tuple-element.11) | copy-start | bytes 1572868

commit v2 on v1

v2 whole, which is shorter than its diff:
```python
import jax
import jax.numpy as jnp
from jax import lax
from jax.experimental import pallas as pl
from jax.experimental.pallas import tpu as pltpu
from jax.sharding import PartitionSpec as P

F32 = jnp.float32
BF16 = jnp.bfloat16
HEAD = 128
QPK = 8
KVH = 4
TOK = 256
LP = 128
NP = 4
HALF = KVH * HEAD
NEG = -1e30
SCALE = HEAD ** -0.5
EXP2_SCALE = SCALE * 1.4426950408889634

NN = (((1,), (0,)), ((), ()))
NT = (((1,), (1,)), ((), ()))


def dot(a, b, dims):
    return lax.dot_general(a, b, dims, preferred_element_type=F32)


def cols(index, width=HEAD):
    return pl.ds(pl.multiple_of(index * width, width), width)


def build_masks(len_ref, prm_ref, bias, qmask, lmask):
    def slot_ids(place):
        resp = jnp.full(place.shape, -1, jnp.int32)
        prompt = jnp.full(place.shape, -1, jnp.int32)
        start = jnp.int32(0)
        for i in range(4):
            end = start + len_ref[0, i]
            inside = (place >= start) & (place < end)
            resp = jnp.where(inside, i, resp)
            prompt = jnp.where(inside, prm_ref[0, i], prompt)
            start = end
        return resp, prompt

    keys = lax.broadcasted_iota(jnp.int32, (TOK, TOK), 0)
    slots = lax.broadcasted_iota(jnp.int32, (TOK, TOK), 1)
    key_resp, _ = slot_ids(keys)
    slot_resp, _ = slot_ids(slots)
    allowed = (key_resp == slot_resp) & (keys <= slots) & (slot_resp >= 0)
    bias[...] = jnp.where(allowed, 0.0, NEG)
    _, by_row = slot_ids(lax.broadcasted_iota(jnp.int32, (TOK, HEAD), 0))
    _, by_lane = slot_ids(lax.broadcasted_iota(jnp.int32, (LP, TOK), 1))
    for j in range(NP):
        qmask[j] = jnp.where(by_row == j, 1.0, 0.0).astype(BF16)
        lmask[j] = jnp.where(by_lane == j, 1.0, 0.0).astype(BF16)


def self_scores(n, q_ref, do_ref, kv_ref, bias, e_self, dp_self, stat):
    h = n // QPK
    keys = kv_ref[:, cols(h)]
    values = kv_ref[:, cols(h + KVH)]
    raw = dot(keys, q_ref[:, cols(n)], NT) + bias[...]
    top = jnp.max(raw, axis=0, keepdims=True)
    e = jnp.exp2((raw - top) * EXP2_SCALE)
    dp = dot(values, do_ref[:, cols(n)], NT)
    e_self[n] = e
    dp_self[n] = dp
    stat[n, 0:1, :] = top
    stat[n, 1:2, :] = jnp.sum(e, axis=0, keepdims=True)
    stat[n, 2:3, :] = jnp.sum(e * dp, axis=0, keepdims=True)


def prompt_scores(n, q_ref, do_ref, qmask, kvcat, w_pr, ds_pr, stat):
    h = n // QPK
    q = q_ref[:, cols(n)]
    do = do_ref[:, cols(n)]
    qe = jnp.concatenate([q * qmask[j] for j in range(NP)], axis=1)
    de = jnp.concatenate([do * qmask[j] for j in range(NP)], axis=1)
    raw = dot(kvcat[0, h], qe, NT)
    dp = dot(kvcat[1, h], de, NT)
    top_self = stat[n, 0:1, :]
    top = jnp.maximum(jnp.max(raw, axis=0, keepdims=True), top_self)
    e = jnp.exp2((raw - top) * EXP2_SCALE)
    shrink = jnp.exp2((top_self - top) * EXP2_SCALE)
    total = jnp.sum(e, axis=0, keepdims=True) + shrink * stat[n, 1:2, :]
    inverse = 1.0 / total
    delta = (jnp.sum(e * dp, axis=0, keepdims=True) + shrink * stat[n, 2:3, :]) * inverse
    w = e * inverse
    ds = (w * (dp - delta)).astype(BF16)
    w = w.astype(BF16)
    stat[n, 3:4, :] = shrink * inverse
    stat[n, 4:5, :] = delta
    w_pr[n] = w
    ds_pr[n] = ds
    return dot(ds, qe, NN), dot(w, de, NN)


def finish(n, q_ref, do_ref, lmask, kt, vt, e_self, dp_self, w_pr, ds_pr, stat, out_ref, dq_ref):
    h = n // QPK
    w = e_self[n] * stat[n, 3:4, :]
    ds = (w * (dp_self[n] - stat[n, 4:5, :])).astype(BF16)
    w = w.astype(BF16)
    w_all = jnp.concatenate([w_pr[n] * lmask[j] for j in range(NP)] + [w], axis=0)
    ds_all = jnp.concatenate([ds_pr[n] * lmask[j] for j in range(NP)] + [ds], axis=0)
    out = dot(vt[h], w_all, NN).astype(BF16)
    dq = (dot(kt[h], ds_all, NN) * SCALE).astype(BF16)
    out_ref[:, cols(n)] = out.T
    dq_ref[:, cols(n)] = dq.T
    return dot(ds, q_ref[:, cols(n)], NN), dot(w, do_ref[:, cols(n)], NN)


def transposed_tables(kvcat, kv_ref, kt, vt):
    for h in range(KVH):
        for half, table in ((0, kt), (1, vt)):
            for j in range(NP):
                table[h, :, j * LP:(j + 1) * LP] = kvcat[half, h, :, j * HEAD:(j + 1) * HEAD].T
            at = half * HALF + h * HEAD
            table[h, :, NP * LP:] = kv_ref[:, at:at + HEAD].T


N_DP = 8
N_RESP = 16
CH = 16
WIDE = NP * HEAD
HEADS = KVH * QPK
STEP = 2
SELF_CUTS = (0, 10, 20, 32)
FINISH_CUTS = (0, 12, 22, 32)
MESH = pl.DeviceIdType.MESH
SPOTS = sorted(range(1, N_RESP), key=lambda s: -(min(s // 4, 4 - s // 4) + min(s % 4, 4 - s % 4)))
LANES = sorted(range(1, N_DP), key=lambda s: -min(s // 2, 4 - s // 2))


def kernel(
    q_hbm, do_hbm, kv_hbm, slot_ref, len_ref, prm_ref, own_ref,
    out_ref, dq_ref, gr_ref, gp_out,
    q_ref, do_ref, kv_ref,
    bias, qmask, lmask, e_self, dp_self, stat, kvcat, kt, vt, w_pr, ds_pr, dk_acc, dv_acc, dks, dvs,
    buf1, send2, recv2, mine, gp, gland, gmine, gland2, send3, fin, inv,
    in_sem, s1, r1, s2, r2, s3, r3, s4, r4, s5, r5, s6, r6,
):
    a = lax.axis_index("dp")
    c = lax.axis_index("resp")
    x, core = a // 2, lax.rem(a, 2)
    z, y = c // 4, lax.rem(c, 4)

    loads = [
        pltpu.make_async_copy(src, dst, in_sem.at[i])
        for i, (src, dst) in enumerate(((kv_hbm, kv_ref), (q_hbm, q_ref), (do_hbm, do_ref)))
    ]
    for load in loads:
        load.start()

    def col_to(s):
        return lax.rem(z + s // 4, 4) * 4 + lax.rem(y + s % 4, 4)

    def col_from(s):
        return lax.rem(z + 4 - s // 4, 4) * 4 + lax.rem(y + 4 - s % 4, 4)

    def row_to(s):
        return lax.rem(x + s // 2, 4) * 2 + lax.rem(core + s % 2, 2)

    def spot_of(column):
        return lax.rem(z + 4 - jnp.right_shift(column, 2), 4) * 4 + lax.rem(y + 4 - jnp.bitwise_and(column, 3), 4)

    def lane_of(row):
        return lax.rem(x + 4 - jnp.right_shift(row, 1), 4) * 2 + lax.rem(core + 2 - jnp.bitwise_and(row, 1), 2)

    def chunk(index):
        half = index // 8
        block = lax.rem(index, 8)
        return half, pl.ds(pl.multiple_of(block * CH, CH), CH)

    def send(src, dst, ssem, rsem, device):
        return pltpu.make_async_remote_copy(
            src_ref=src, dst_ref=dst, send_sem=ssem, recv_sem=rsem, device_id=device, device_id_type=MESH
        )

    barrier = pltpu.get_barrier_semaphore()
    for s in SPOTS:
        pl.semaphore_signal(barrier, inc=1, device_id=(a, col_to(s)), device_id_type=MESH)
    for s in LANES:
        pl.semaphore_signal(barrier, inc=1, device_id=(row_to(s), c), device_id_type=MESH)
    build_masks(len_ref, prm_ref, bias, qmask, lmask)
    pl.semaphore_wait(barrier, len(SPOTS) + len(LANES))

    my_half, my_rows = chunk(c)

    first = []
    for s in SPOTS:
        to = col_to(s)
        half, rows = chunk(to)
        lanes = pl.ds(pl.multiple_of(half * HALF, HALF), HALF)
        copy = send(slot_ref.at[rows, lanes], buf1.at[s], s1.at[s - 1], r1.at[s - 1], (a, to))
        copy.start()
        first.append(copy)
    buf1[0] = slot_ref[my_rows, pl.ds(pl.multiple_of(my_half * HALF, HALF), HALF)]

    @pl.loop(0, N_RESP)
    def _(s):
        device = a * N_RESP + lax.rem(z + s // 4, 4) * 4 + lax.rem(y + lax.rem(s, 4), 4)
        found = jnp.int32(-1)
        for k in range(N_DP * NP):
            found = jnp.where(own_ref[k % NP, k // NP] == device, k, found)
        inv[s] = found

    for load in loads:
        load.wait()

    def self_part(lo, hi):
        @pl.loop(lo // STEP, hi // STEP)
        def _(i):
            for u in range(STEP):
                self_scores(i * STEP + u, q_ref, do_ref, kv_ref, bias, e_self, dp_self, stat)

    self_part(SELF_CUTS[0], SELF_CUTS[1])

    for copy in first:
        copy.wait_recv()
    second = []
    for s in LANES + [0]:
        to = row_to(s)
        for j in range(NP):
            piece = buf1[spot_of(jnp.bitwise_and(own_ref[j, to], N_RESP - 1))]
            if s == 0:
                recv2[0, j] = piece
            else:
                send2[s - 1, j] = piece
        if s:
            copy = send(send2.at[s - 1], recv2.at[s], s2.at[s - 1], r2.at[s - 1], (to, c))
            copy.start()
            second.append(copy)

    self_part(SELF_CUTS[1], SELF_CUTS[2])

    for copy in second:
        copy.wait_recv()
    for j in range(NP):
        piece = recv2[lane_of(jnp.right_shift(own_ref[j, a], 4)), j]
        for h in range(KVH):
            mine[h, :, j * HEAD:(j + 1) * HEAD] = piece[:, h * HEAD:(h + 1) * HEAD]
    third = []
    for h in range(KVH):
        kvcat[my_half, h, my_rows, :] = mine[h]
        for s in SPOTS:
            copy = send(
                mine.at[h], kvcat.at[my_half, h, my_rows, :], s3.at[h, s - 1], r3.at[h, s - 1], (a, col_to(s))
            )
            copy.start()
            third.append(copy)

    self_part(SELF_CUTS[2], SELF_CUTS[3])

    fourth = []
    for h in range(KVH):
        for s in SPOTS:
            half, rows = chunk(col_from(s))
            send(mine.at[h], kvcat.at[half, h, rows, :], s3.at[h, s - 1], r3.at[h, s - 1], (a, col_to(s))).wait_recv()
        dk_acc[...] = jnp.zeros_like(dk_acc)
        dv_acc[...] = jnp.zeros_like(dv_acc)

        @pl.loop(0, QPK // STEP)
        def _(i):
            parts = [
                prompt_scores(h * QPK + i * STEP + u, q_ref, do_ref, qmask, kvcat, w_pr, ds_pr, stat)
                for u in range(STEP)
            ]
            dk_acc[...] += sum(p[0] for p in parts)
            dv_acc[...] += sum(p[1] for p in parts)

        gp[h, 0] = (dk_acc[...] * SCALE).astype(BF16)
        gp[h, 1] = dv_acc[...].astype(BF16)
        for s in SPOTS:
            to = col_to(s)
            half, rows = chunk(to)
            copy = send(gp.at[h, half, rows, :], gland.at[s - 1, h], s4.at[h, s - 1], r4.at[h, s - 1], (a, to))
            copy.start()
            fourth.append(copy)

    transposed_tables(kvcat, kv_ref, kt, vt)
    dks[...] = jnp.zeros_like(dks)
    dvs[...] = jnp.zeros_like(dvs)

    def finish_part(lo, hi):
        @pl.loop(lo // STEP, hi // STEP)
        def _(i):
            parts = [
                finish(i * STEP + u, q_ref, do_ref, lmask, kt, vt, e_self, dp_self, w_pr, ds_pr, stat, out_ref, dq_ref)
                for u in range(STEP)
            ]
            h = i * STEP // QPK
            dks[h] += sum(p[0] for p in parts)
            dvs[h] += sum(p[1] for p in parts)

    finish_part(FINISH_CUTS[0], FINISH_CUTS[1])

    for copy in fourth:
        copy.wait_recv()
    for h in range(KVH):
        total = gp[h, my_half, my_rows, :].astype(F32)
        for s in SPOTS:
            total += gland[s - 1, h].astype(F32)
        total = total.astype(BF16)
        for j in range(NP):
            gmine[j, h] = total[:, j * HEAD:(j + 1) * HEAD]
    gland2[0] = gmine[...]
    fifth = []
    for s in LANES:
        copy = send(gmine, gland2.at[s], s5.at[s - 1], r5.at[s - 1], (row_to(s), c))
        copy.start()
        fifth.append(copy)

    finish_part(FINISH_CUTS[1], FINISH_CUTS[2])

    for copy in fifth:
        copy.wait_recv()
    sixth = []
    for s in SPOTS + [0]:
        index = inv[s]
        at = jnp.maximum(index, 0)
        piece = gland2[lane_of(jnp.right_shift(at, 2)), jnp.bitwise_and(at, 3)].astype(F32)
        piece = jnp.where(index >= 0, piece, 0.0).astype(BF16)
        if s == 0:
            fin[0] = piece
        else:
            send3[s - 1] = piece
            copy = send(send3.at[s - 1], fin.at[s], s6.at[s - 1], r6.at[s - 1], (a, col_to(s)))
            copy.start()
            sixth.append(copy)

    finish_part(FINISH_CUTS[2], FINISH_CUTS[3])

    for h in range(KVH):
        gr_ref[:, h * HEAD:(h + 1) * HEAD] = (dks[h] * SCALE).astype(BF16)
        gr_ref[:, HALF + h * HEAD:HALF + (h + 1) * HEAD] = dvs[h].astype(BF16)

    for copy in sixth:
        copy.wait_recv()
    for s in range(N_RESP):
        half, rows = chunk(col_from(s))
        for h in range(KVH):
            lanes = pl.ds(pl.multiple_of(half * HALF + h * HEAD, HEAD), HEAD)
            gp_out[rows, lanes] = fin[s, h].astype(F32)

    for copy in first + second + third + fourth + fifth + sixth:
        copy.wait_send()


def local(queries, response_kv, cotangent, prompt_kv, resp_lengths, resp_prompt, owners):
    vm = pl.BlockSpec(memory_space=pltpu.VMEM)
    sm = pl.BlockSpec(memory_space=pltpu.SMEM)
    hbm = pl.BlockSpec(memory_space=pl.ANY)
    peers = (N_RESP - 1,)
    row_peers = (N_DP - 1,)
    dma = pltpu.SemaphoreType.DMA
    outs = pl.pallas_call(
        kernel,
        in_specs=[hbm, hbm, hbm, vm, sm, sm, sm],
        out_specs=[vm] * 4,
        out_shape=[
            pltpu.VMEM((TOK, 4096), BF16),
            pltpu.VMEM((TOK, 4096), BF16),
            pltpu.VMEM((TOK, 1024), BF16),
            pltpu.VMEM((LP, 1024), F32),
        ],
        scratch_shapes=[
            pltpu.VMEM((TOK, 4096), BF16),
            pltpu.VMEM((TOK, 4096), BF16),
            pltpu.VMEM((TOK, 1024), BF16),
            pltpu.VMEM((TOK, TOK), F32),
            pltpu.VMEM((NP, TOK, HEAD), BF16),
            pltpu.VMEM((NP, LP, TOK), BF16),
            pltpu.VMEM((HEADS, TOK, TOK), F32),
            pltpu.VMEM((HEADS, TOK, TOK), F32),
            pltpu.VMEM((HEADS, 8, TOK), F32),
            pltpu.VMEM((2, KVH, LP, WIDE), BF16),
            pltpu.VMEM((KVH, HEAD, NP * LP + TOK), BF16),
            pltpu.VMEM((KVH, HEAD, NP * LP + TOK), BF16),
            pltpu.VMEM((HEADS, LP, TOK), BF16),
            pltpu.VMEM((HEADS, LP, TOK), BF16),
            pltpu.VMEM((LP, WIDE), F32),
            pltpu.VMEM((LP, WIDE), F32),
            pltpu.VMEM((KVH, TOK, HEAD), F32),
            pltpu.VMEM((KVH, TOK, HEAD), F32),
            pltpu.VMEM((N_RESP, CH, HALF), BF16),
            pltpu.VMEM((N_DP - 1, NP, CH, HALF), BF16),
            pltpu.VMEM((N_DP, NP, CH, HALF), BF16),
            pltpu.VMEM((KVH, CH, WIDE), BF16),
            pltpu.VMEM((KVH, 2, LP, WIDE), BF16),
            pltpu.VMEM((N_RESP - 1, KVH, CH, WIDE), BF16),
            pltpu.VMEM((NP, KVH, CH, HEAD), BF16),
            pltpu.VMEM((N_DP, NP, KVH, CH, HEAD), BF16),
            pltpu.VMEM((N_RESP - 1, KVH, CH, HEAD), BF16),
            pltpu.VMEM((N_RESP, KVH, CH, HEAD), BF16),
            pltpu.SMEM((N_RESP,), jnp.int32),
            dma((3,)),
            dma(peers), dma(peers),
            dma(row_peers), dma(row_peers),
            dma((KVH,) + peers), dma((KVH,) + peers),
            dma((KVH,) + peers), dma((KVH,) + peers),
            dma(row_peers), dma(row_peers),
            dma(peers), dma(peers),
        ],
        compiler_params=pltpu.CompilerParams(
            collective_id=0, has_side_effects=True, vmem_limit_bytes=50 * 2 ** 20
        ),
        name="grouped_attention",
    )(
        queries[0], cotangent[0], response_kv[0], prompt_kv[0, 0],
        resp_lengths[0], resp_prompt[0], owners.T,
    )
    attn_out, grad_queries, grad_response, grad_prompt = outs
    return attn_out[None], grad_queries[None], grad_response[None], grad_prompt[None, None]


def solution(mesh):
    placed = (
        P("dp", "resp", None),
        P("dp", "resp", None),
        P("dp", "resp", None),
        P("dp", "resp", None, None),
        P("dp", "resp", None),
        P("dp", "resp", None),
        P(),
    )
    return jax.shard_map(
        local,
        mesh=mesh,
        in_specs=placed,
        out_specs=(
            P("dp", "resp", None),
            P("dp", "resp", None),
            P("dp", "resp", None),
            P("dp", "resp", None, None),
        ),
        check_vma=False,
    )
```

time: 83.3 us -> 67.8 us (0.81)
  Pallas kernels: 74.9 us -> 62.8 us
  local copies, waits for them, and re-layouts: 7.59 us -> 4.23 us
    pallas_call x1, Pallas kernels: 74.9 us -> 62.8 us  [local(): pl.pallas_call(kernel, in_specs=[hbm, hbm, hbm, vm, sm, sm, sm], out_spec...]
    unnamed x11 -> x4, local copies, waits for them, and re-layouts: 7.59 us -> 4.23 us
where the time goes in v2:
time: 67.8 us; the launch traced here: 67.7 us
  Pallas kernels  62.8 us (93%)
  local copies, waits for them, and re-layouts  4.23 us (6%)
    pallas_call x1, Pallas kernels, local(): pl.pallas_call(kernel, in_specs=[hbm, hbm, hbm, vm, sm, sm, sm], out_spec...  62.8 us
    unnamed x4, local copies, waits for them, and re-layouts  4.23 us

profile of v2, /device:TPU:1, one launch (start us, length us, event | category | flops | bytes accessed | tf_op | source)
XLA Modules:
  0.0 67.7 jit_solution(257806803718155755)
XLA Ops:
  0.6 62.8 %grouped_attention.1 = (bf16[256,4096]{1,0:T(8,128)(2,1)S(1)}, bf16[256,4096]{1,0:T(8,128)(2,1)S(1)}, bf16[256,1024]{1,0:T(8,128)(2,1)S(1)}, f32[128,1024]{1,0:T(8,128)S(1)}) custom-call(bf16[256,4096]{1,0:T(8,128)(2,1)} %bitcast.15, bf16[256,4096]{1,0:T(8,128)(2,1)} %bitcast.16, bf16[256,1024]{1,0:T(8,128)(2,1)} %bitcast.17, bf16[128,1024]{1,0:T(8,128)(2,1)} %bitcast.18, ...), custom_call_target="tpu_custom_call" | custom-call | tf_op jit(solution)/shard_map/grouped_attention/pallas_call | solution.py:357
  63.5 1.3 %copy.15 = bf16[1,256,4096]{2,1,0:T(8,128)(2,1)} copy(bf16[1,256,4096]{2,1,0:T(8,128)(2,1)S(1)} %bitcast.12) | data formatting | bytes 4194304
  64.8 1.3 %copy.16 = bf16[1,256,4096]{2,1,0:T(8,128)(2,1)} copy(bf16[1,256,4096]{2,1,0:T(8,128)(2,1)S(1)} %bitcast.11) | data formatting | bytes 4194304
  66.1 0.8 %copy.17 = bf16[1,256,1024]{2,1,0:T(8,128)(2,1)} copy(bf16[1,256,1024]{2,1,0:T(8,128)(2,1)S(1)} %bitcast.14) | data formatting | bytes 1048576
  66.9 0.8 %copy.18 = f32[1,1,128,1024]{3,2,1,0:T(8,128)} copy(f32[1,1,128,1024]{3,2,1,0:T(8,128)S(1)} %bitcast.13) | data formatting | bytes 1048576

commit v3 on v2

--- a/solution.py
+++ b/solution.py
@@ -19,7 +19,6 @@
 EXP2_SCALE = SCALE * 1.4426950408889634
 
 NN = (((1,), (0,)), ((), ()))
-NT = (((1,), (1,)), ((), ()))
 
 
 def dot(a, b, dims):
@@ -56,14 +55,18 @@
         lmask[j] = jnp.where(by_lane == j, 1.0, 0.0).astype(BF16)
 
 
-def self_scores(n, q_ref, do_ref, kv_ref, bias, e_self, dp_self, stat):
+def self_scores(n, q_ref, do_ref, kv_ref, bias, qt, dt, e_self, dp_self, stat):
     h = n // QPK
     keys = kv_ref[:, cols(h)]
     values = kv_ref[:, cols(h + KVH)]
-    raw = dot(keys, q_ref[:, cols(n)], NT) + bias[...]
+    q = q_ref[:, cols(n)].T
+    do = do_ref[:, cols(n)].T
+    qt[n] = q
+    dt[n] = do
+    raw = dot(keys, q, NN) + bias[...]
     top = jnp.max(raw, axis=0, keepdims=True)
     e = jnp.exp2((raw - top) * EXP2_SCALE)
-    dp = dot(values, do_ref[:, cols(n)], NT)
+    dp = dot(values, do, NN)
     e_self[n] = e
     dp_self[n] = dp
     stat[n, 0:1, :] = top
@@ -71,14 +74,14 @@
     stat[n, 2:3, :] = jnp.sum(e * dp, axis=0, keepdims=True)
 
 
-def prompt_scores(n, q_ref, do_ref, qmask, kvcat, w_pr, ds_pr, stat):
+def prompt_scores(n, q_ref, do_ref, qt, dt, qmask, lmask, kvcat, w_pr, ds_pr, stat):
     h = n // QPK
     q = q_ref[:, cols(n)]
     do = do_ref[:, cols(n)]
     qe = jnp.concatenate([q * qmask[j] for j in range(NP)], axis=1)
     de = jnp.concatenate([do * qmask[j] for j in range(NP)], axis=1)
-    raw = dot(kvcat[0, h], qe, NT)
-    dp = dot(kvcat[1, h], de, NT)
+    raw = dot(kvcat[0, h], jnp.concatenate([qt[n] * lmask[j] for j in range(NP)], axis=0), NN)
+    dp = dot(kvcat[1, h], jnp.concatenate([dt[n] * lmask[j] for j in range(NP)], axis=0), NN)
     top_self = stat[n, 0:1, :]
     top = jnp.maximum(jnp.max(raw, axis=0, keepdims=True), top_self)
     e = jnp.exp2((raw - top) * EXP2_SCALE)
@@ -124,9 +127,12 @@
 CH = 16
 WIDE = NP * HEAD
 HEADS = KVH * QPK
-STEP = 2
-SELF_CUTS = (0, 10, 20, 32)
-FINISH_CUTS = (0, 12, 22, 32)
+SELF_STEP = 4
+PROMPT_STEP = 2
+FINISH_STEP = 4
+SELF_CUTS = (0, 8, 16, 20, 24, 28, 32)
+FINISH_CUTS = (0, 8, 12, 16, 20, 24, 32)
+PAIRS = 2
 MESH = pl.DeviceIdType.MESH
 SPOTS = sorted(range(1, N_RESP), key=lambda s: -(min(s // 4, 4 - s // 4) + min(s % 4, 4 - s % 4)))
 LANES = sorted(range(1, N_DP), key=lambda s: -min(s // 2, 4 - s // 2))
@@ -136,10 +142,12 @@
     q_hbm, do_hbm, kv_hbm, slot_ref, len_ref, prm_ref, own_ref,
     out_ref, dq_ref, gr_ref, gp_out,
     q_ref, do_ref, kv_ref,
-    bias, qmask, lmask, e_self, dp_self, stat, kvcat, kt, vt, w_pr, ds_pr, dk_acc, dv_acc, dks, dvs,
-    buf1, send2, recv2, mine, gp, gland, gmine, gland2, send3, fin, inv,
+    bias, qmask, lmask, qt, dt, e_self, dp_self, stat, kvcat, kt, vt, w_pr, ds_pr, dk_acc, dv_acc, dks, dvs,
+    buf1, send2, got_a, got_b, got_c, got_d, mine, gp, gland, gmine, back_a, back_b, back_c, back_d, send3, fin, inv,
     in_sem, s1, r1, s2, r2, s3, r3, s4, r4, s5, r5, s6, r6,
 ):
+    recv2 = (got_a, got_b, got_c, got_d)
+    gland2 = (back_a, back_b, back_c, back_d)
     a = lax.axis_index("dp")
     c = lax.axis_index("resp")
     x, core = a // 2, lax.rem(a, 2)
@@ -200,57 +208,61 @@
     @pl.loop(0, N_RESP)
     def _(s):
         device = a * N_RESP + lax.rem(z + s // 4, 4) * 4 + lax.rem(y + lax.rem(s, 4), 4)
-        found = jnp.int32(-1)
-        for k in range(N_DP * NP):
-            found = jnp.where(own_ref[k % NP, k // NP] == device, k, found)
-        inv[s] = found
+        found = [jnp.where(own_ref[k % NP, k // NP] == device, k + 1, 0) for k in range(N_DP * NP)]
+        while len(found) > 1:
+            found = [jnp.maximum(found[k], found[k + 1]) for k in range(0, len(found), 2)]
+        inv[s] = found[0]
 
     for load in loads:
         load.wait()
 
     def self_part(lo, hi):
-        @pl.loop(lo // STEP, hi // STEP)
+        @pl.loop(lo // SELF_STEP, hi // SELF_STEP)
         def _(i):
-            for u in range(STEP):
-                self_scores(i * STEP + u, q_ref, do_ref, kv_ref, bias, e_self, dp_self, stat)
+            for u in range(SELF_STEP):
+                self_scores(i * SELF_STEP + u, q_ref, do_ref, kv_ref, bias, qt, dt, e_self, dp_self, stat)
 
     self_part(SELF_CUTS[0], SELF_CUTS[1])
 
     for copy in first:
         copy.wait_recv()
     second = []
-    for s in LANES + [0]:
-        to = row_to(s)
+    spots = {
+        (s, j): spot_of(jnp.bitwise_and(own_ref[j, row_to(s)], N_RESP - 1)) for s in range(N_DP) for j in range(NP)
+    }
+    for h in range(KVH):
+        for s in LANES + [0]:
+            for j in range(NP):
+                piece = buf1[spots[s, j], :, h * HEAD:(h + 1) * HEAD]
+                if s == 0:
+                    recv2[h][0, :, j * HEAD:(j + 1) * HEAD] = piece
+                else:
+                    send2[h, s - 1, :, j * HEAD:(j + 1) * HEAD] = piece
+            if s:
+                copy = send(
+                    send2.at[h, s - 1], recv2[h].at[s], s2.at[h, s - 1], r2.at[h, s - 1], (row_to(s), c)
+                )
+                copy.start()
+                second.append(copy)
+
+    self_part(SELF_CUTS[1], SELF_CUTS[2])
+
+    from_lane = [lane_of(jnp.right_shift(own_ref[j, a], 4)) for j in range(NP)]
+    third = []
+    for h in range(KVH):
+        for copy in second[h * len(LANES):(h + 1) * len(LANES)]:
+            copy.wait_recv()
         for j in range(NP):
-            piece = buf1[spot_of(jnp.bitwise_and(own_ref[j, to], N_RESP - 1))]
-            if s == 0:
-                recv2[0, j] = piece
-            else:
-                send2[s - 1, j] = piece
-        if s:
-            copy = send(send2.at[s - 1], recv2.at[s], s2.at[s - 1], r2.at[s - 1], (to, c))
-            copy.start()
-            second.append(copy)
-
-    self_part(SELF_CUTS[1], SELF_CUTS[2])
-
-    for copy in second:
-        copy.wait_recv()
-    for j in range(NP):
-        piece = recv2[lane_of(jnp.right_shift(own_ref[j, a], 4)), j]
-        for h in range(KVH):
-            mine[h, :, j * HEAD:(j + 1) * HEAD] = piece[:, h * HEAD:(h + 1) * HEAD]
-    third = []
-    for h in range(KVH):
-        kvcat[my_half, h, my_rows, :] = mine[h]
+            at = slice(j * HEAD, (j + 1) * HEAD)
+            mine[h, :, at] = recv2[h][from_lane[j], :, at]
         for s in SPOTS:
             copy = send(
                 mine.at[h], kvcat.at[my_half, h, my_rows, :], s3.at[h, s - 1], r3.at[h, s - 1], (a, col_to(s))
             )
             copy.start()
             third.append(copy)
-
-    self_part(SELF_CUTS[2], SELF_CUTS[3])
+        kvcat[my_half, h, my_rows, :] = mine[h]
+        self_part(SELF_CUTS[2 + h], SELF_CUTS[3 + h])
 
     fourth = []
     for h in range(KVH):
@@ -260,11 +272,13 @@
         dk_acc[...] = jnp.zeros_like(dk_acc)
         dv_acc[...] = jnp.zeros_like(dv_acc)
 
-        @pl.loop(0, QPK // STEP)
+        @pl.loop(0, QPK // PROMPT_STEP)
         def _(i):
             parts = [
-                prompt_scores(h * QPK + i * STEP + u, q_ref, do_ref, qmask, kvcat, w_pr, ds_pr, stat)
-                for u in range(STEP)
+                prompt_scores(
+                    h * QPK + i * PROMPT_STEP + u, q_ref, do_ref, qt, dt, qmask, lmask, kvcat, w_pr, ds_pr, stat
+                )
+                for u in range(PROMPT_STEP)
             ]
             dk_acc[...] += sum(p[0] for p in parts)
             dv_acc[...] += sum(p[1] for p in parts)
@@ -283,53 +297,59 @@
     dvs[...] = jnp.zeros_like(dvs)
 
     def finish_part(lo, hi):
-        @pl.loop(lo // STEP, hi // STEP)
+        @pl.loop(lo // FINISH_STEP, hi // FINISH_STEP)
         def _(i):
             parts = [
-                finish(i * STEP + u, q_ref, do_ref, lmask, kt, vt, e_self, dp_self, w_pr, ds_pr, stat, out_ref, dq_ref)
-                for u in range(STEP)
+                finish(i * FINISH_STEP + u, q_ref, do_ref, lmask, kt, vt, e_self, dp_self, w_pr, ds_pr, stat, out_ref, dq_ref)
+                for u in range(FINISH_STEP)
             ]
-            h = i * STEP // QPK
+            h = i * FINISH_STEP // QPK
             dks[h] += sum(p[0] for p in parts)
             dvs[h] += sum(p[1] for p in parts)
 
-    finish_part(FINISH_CUTS[0], FINISH_CUTS[1])
-
-    for copy in fourth:
-        copy.wait_recv()
-    for h in range(KVH):
+    fifth = []
+    sixth = []
+
+    def to_owners(p):
+        for copy in fifth[p * PAIRS * len(LANES):(p + 1) * PAIRS * len(LANES)]:
+            copy.wait_recv()
+        for s in SPOTS + [0]:
+            number = inv[s]
+            at = jnp.maximum(number - 1, 0)
+            lane = lane_of(jnp.right_shift(at, 2))
+            j = jnp.bitwise_and(at, 3)
+            for u in range(PAIRS):
+                piece = gland2[p * PAIRS + u][lane, j].astype(F32)
+                piece = jnp.where(number > 0, piece, 0.0).astype(BF16)
+                if s == 0:
+                    fin[p, 0, u] = piece
+                else:
+                    send3[p, s - 1, u] = piece
+            if s:
+                copy = send(send3.at[p, s - 1], fin.at[p, s], s6.at[p, s - 1], r6.at[p, s - 1], (a, col_to(s)))
+                copy.start()
+                sixth.append(copy)
+
+    for h in range(KVH):
+        finish_part(FINISH_CUTS[h], FINISH_CUTS[h + 1])
+        for copy in fourth[h * len(SPOTS):(h + 1) * len(SPOTS)]:
+            copy.wait_recv()
         total = gp[h, my_half, my_rows, :].astype(F32)
         for s in SPOTS:
             total += gland[s - 1, h].astype(F32)
         total = total.astype(BF16)
         for j in range(NP):
-            gmine[j, h] = total[:, j * HEAD:(j + 1) * HEAD]
-    gland2[0] = gmine[...]
-    fifth = []
-    for s in LANES:
-        copy = send(gmine, gland2.at[s], s5.at[s - 1], r5.at[s - 1], (row_to(s), c))
-        copy.start()
-        fifth.append(copy)
-
-    finish_part(FINISH_CUTS[1], FINISH_CUTS[2])
-
-    for copy in fifth:
-        copy.wait_recv()
-    sixth = []
-    for s in SPOTS + [0]:
-        index = inv[s]
-        at = jnp.maximum(index, 0)
-        piece = gland2[lane_of(jnp.right_shift(at, 2)), jnp.bitwise_and(at, 3)].astype(F32)
-        piece = jnp.where(index >= 0, piece, 0.0).astype(BF16)
-        if s == 0:
-            fin[0] = piece
-        else:
-            send3[s - 1] = piece
-            copy = send(send3.at[s - 1], fin.at[s], s6.at[s - 1], r6.at[s - 1], (a, col_to(s)))
+            gmine[h, j] = total[:, j * HEAD:(j + 1) * HEAD]
+        for s in LANES:
+            copy = send(gmine.at[h], gland2[h].at[s], s5.at[h, s - 1], r5.at[h, s - 1], (row_to(s), c))
             copy.start()
-            sixth.append(copy)
-
-    finish_part(FINISH_CUTS[2], FINISH_CUTS[3])
+            fifth.append(copy)
+        gland2[h][0] = gmine[h]
+        if h == KVH - 1:
+            to_owners(0)
+    finish_part(FINISH_CUTS[4], FINISH_CUTS[5])
+    to_owners(1)
+    finish_part(FINISH_CUTS[5], FINISH_CUTS[6])
 
     for h in range(KVH):
         gr_ref[:, h * HEAD:(h + 1) * HEAD] = (dks[h] * SCALE).astype(BF16)
@@ -341,7 +361,7 @@
         half, rows = chunk(col_from(s))
         for h in range(KVH):
             lanes = pl.ds(pl.multiple_of(half * HALF + h * HEAD, HEAD), HEAD)
-            gp_out[rows, lanes] = fin[s, h].astype(F32)
+            gp_out[rows, lanes] = fin[h // PAIRS, s, h % PAIRS].astype(F32)
 
     for copy in first + second + third + fourth + fifth + sixth:
         copy.wait_send()
@@ -371,6 +391,8 @@
             pltpu.VMEM((TOK, TOK), F32),
             pltpu.VMEM((NP, TOK, HEAD), BF16),
             pltpu.VMEM((NP, LP, TOK), BF16),
+            pltpu.VMEM((HEADS, HEAD, TOK), BF16),
+            pltpu.VMEM((HEADS, HEAD, TOK), BF16),
             pltpu.VMEM((HEADS, TOK, TOK), F32),
             pltpu.VMEM((HEADS, TOK, TOK), F32),
             pltpu.VMEM((HEADS, 8, TOK), F32),
@@ -384,23 +406,23 @@
             pltpu.VMEM((KVH, TOK, HEAD), F32),
             pltpu.VMEM((KVH, TOK, HEAD), F32),
             pltpu.VMEM((N_RESP, CH, HALF), BF16),
-            pltpu.VMEM((N_DP - 1, NP, CH, HALF), BF16),
-            pltpu.VMEM((N_DP, NP, CH, HALF), BF16),
+            pltpu.VMEM((KVH, N_DP - 1, CH, WIDE), BF16),
+            *[pltpu.VMEM((N_DP, CH, WIDE), BF16)] * KVH,
             pltpu.VMEM((KVH, CH, WIDE), BF16),
             pltpu.VMEM((KVH, 2, LP, WIDE), BF16),
             pltpu.VMEM((N_RESP - 1, KVH, CH, WIDE), BF16),
-            pltpu.VMEM((NP, KVH, CH, HEAD), BF16),
-            pltpu.VMEM((N_DP, NP, KVH, CH, HEAD), BF16),
-            pltpu.VMEM((N_RESP - 1, KVH, CH, HEAD), BF16),
-            pltpu.VMEM((N_RESP, KVH, CH, HEAD), BF16),
+            pltpu.VMEM((KVH, NP, CH, HEAD), BF16),
+            *[pltpu.VMEM((N_DP, NP, CH, HEAD), BF16)] * KVH,
+            pltpu.VMEM((KVH // PAIRS, N_RESP - 1, PAIRS, CH, HEAD), BF16),
+            pltpu.VMEM((KVH // PAIRS, N_RESP, PAIRS, CH, HEAD), BF16),
             pltpu.SMEM((N_RESP,), jnp.int32),
             dma((3,)),
             dma(peers), dma(peers),
-            dma(row_peers), dma(row_peers),
+            dma((KVH,) + row_peers), dma((KVH,) + row_peers),
             dma((KVH,) + peers), dma((KVH,) + peers),
             dma((KVH,) + peers), dma((KVH,) + peers),
-            dma(row_peers), dma(row_peers),
-            dma(peers), dma(peers),
+            dma((KVH,) + row_peers), dma((KVH,) + row_peers),
+            dma((KVH // PAIRS,) + peers), dma((KVH // PAIRS,) + peers),
         ],
         compiler_params=pltpu.CompilerParams(
             collective_id=0, has_side_effects=True, vmem_limit_bytes=50 * 2 ** 20

time: 67.8 us -> 62.3 us (0.919)
  Pallas kernels: 62.8 us -> 57.3 us
    pallas_call x1, Pallas kernels: 62.8 us -> 57.3 us  [local(): pl.pallas_call(kernel, in_specs=[hbm, hbm, hbm, vm, sm, sm, sm], out_spec...]
where the time goes in v3:
time: 62.3 us; the launch traced here: 62.2 us
  Pallas kernels  57.3 us (92%)
  local copies, waits for them, and re-layouts  4.23 us (7%)
  between operations  0.64 us (1%)
    pallas_call x1, Pallas kernels, local(): pl.pallas_call(kernel, in_specs=[hbm, hbm, hbm, vm, sm, sm, sm], out_spec...  57.3 us
    unnamed x4, local copies, waits for them, and re-layouts  4.23 us

profile of v3, /device:TPU:1, one launch (start us, length us, event | category | flops | bytes accessed | tf_op | source)
XLA Modules:
  0.0 62.2 jit_solution(8400073752201726095)
XLA Ops:
  0.6 57.3 %grouped_attention.1 = (bf16[256,4096]{1,0:T(8,128)(2,1)S(1)}, bf16[256,4096]{1,0:T(8,128)(2,1)S(1)}, bf16[256,1024]{1,0:T(8,128)(2,1)S(1)}, f32[128,1024]{1,0:T(8,128)S(1)}) custom-call(bf16[256,4096]{1,0:T(8,128)(2,1)} %bitcast.15, bf16[256,4096]{1,0:T(8,128)(2,1)} %bitcast.16, bf16[256,1024]{1,0:T(8,128)(2,1)} %bitcast.17, bf16[128,1024]{1,0:T(8,128)(2,1)} %bitcast.18, ...), custom_call_target="tpu_custom_call" | custom-call | tf_op jit(solution)/shard_map/grouped_attention/pallas_call | solution.py:377
  58.0 1.3 %copy.15 = bf16[1,256,4096]{2,1,0:T(8,128)(2,1)} copy(bf16[1,256,4096]{2,1,0:T(8,128)(2,1)S(1)} %bitcast.12) | data formatting | bytes 4194304
  59.3 1.3 %copy.16 = bf16[1,256,4096]{2,1,0:T(8,128)(2,1)} copy(bf16[1,256,4096]{2,1,0:T(8,128)(2,1)S(1)} %bitcast.11) | data formatting | bytes 4194304
  60.6 0.8 %copy.17 = bf16[1,256,1024]{2,1,0:T(8,128)(2,1)} copy(bf16[1,256,1024]{2,1,0:T(8,128)(2,1)S(1)} %bitcast.14) | data formatting | bytes 1048576
  61.4 0.8 %copy.18 = f32[1,1,128,1024]{3,2,1,0:T(8,128)} copy(f32[1,1,128,1024]{3,2,1,0:T(8,128)S(1)} %bitcast.13) | data formatting | bytes 1048576

commit v4 on v3

--- a/solution.py
+++ b/solution.py
@@ -185,6 +185,12 @@
             src_ref=src, dst_ref=dst, send_sem=ssem, recv_sem=rsem, device_id=device, device_id_type=MESH
         )
 
+    def arrived(ref, rsem):
+        send(ref, ref, s1, rsem, (a, col_to(1))).wait_recv()
+
+    def gone(ref, ssem):
+        send(ref, ref, ssem, r1, (a, col_to(1))).wait_send()
+
     barrier = pltpu.get_barrier_semaphore()
     for s in SPOTS:
         pl.semaphore_signal(barrier, inc=1, device_id=(a, col_to(s)), device_id_type=MESH)
@@ -195,14 +201,12 @@
 
     my_half, my_rows = chunk(c)
 
-    first = []
     for s in SPOTS:
         to = col_to(s)
         half, rows = chunk(to)
         lanes = pl.ds(pl.multiple_of(half * HALF, HALF), HALF)
-        copy = send(slot_ref.at[rows, lanes], buf1.at[s], s1.at[s - 1], r1.at[s - 1], (a, to))
+        copy = send(slot_ref.at[rows, lanes], buf1.at[s], s1, r1, (a, to))
         copy.start()
-        first.append(copy)
     buf1[0] = slot_ref[my_rows, pl.ds(pl.multiple_of(my_half * HALF, HALF), HALF)]
 
     @pl.loop(0, N_RESP)
@@ -224,9 +228,7 @@
 
     self_part(SELF_CUTS[0], SELF_CUTS[1])
 
-    for copy in first:
-        copy.wait_recv()
-    second = []
+    arrived(buf1.at[pl.ds(1, N_RESP - 1)], r1)
     spots = {
         (s, j): spot_of(jnp.bitwise_and(own_ref[j, row_to(s)], N_RESP - 1)) for s in range(N_DP) for j in range(NP)
     }
@@ -239,36 +241,25 @@
                 else:
                     send2[h, s - 1, :, j * HEAD:(j + 1) * HEAD] = piece
             if s:
-                copy = send(
-                    send2.at[h, s - 1], recv2[h].at[s], s2.at[h, s - 1], r2.at[h, s - 1], (row_to(s), c)
-                )
+                copy = send(send2.at[h, s - 1], recv2[h].at[s], s2, r2.at[h], (row_to(s), c))
                 copy.start()
-                second.append(copy)
 
     self_part(SELF_CUTS[1], SELF_CUTS[2])
 
     from_lane = [lane_of(jnp.right_shift(own_ref[j, a], 4)) for j in range(NP)]
-    third = []
-    for h in range(KVH):
-        for copy in second[h * len(LANES):(h + 1) * len(LANES)]:
-            copy.wait_recv()
+    for h in range(KVH):
+        arrived(recv2[h].at[pl.ds(1, N_DP - 1)], r2.at[h])
         for j in range(NP):
             at = slice(j * HEAD, (j + 1) * HEAD)
             mine[h, :, at] = recv2[h][from_lane[j], :, at]
         for s in SPOTS:
-            copy = send(
-                mine.at[h], kvcat.at[my_half, h, my_rows, :], s3.at[h, s - 1], r3.at[h, s - 1], (a, col_to(s))
-            )
+            copy = send(mine.at[h], kvcat.at[my_half, h, my_rows, :], s3, r3.at[h], (a, col_to(s)))
             copy.start()
-            third.append(copy)
         kvcat[my_half, h, my_rows, :] = mine[h]
         self_part(SELF_CUTS[2 + h], SELF_CUTS[3 + h])
 
-    fourth = []
-    for h in range(KVH):
-        for s in SPOTS:
-            half, rows = chunk(col_from(s))
-            send(mine.at[h], kvcat.at[half, h, rows, :], s3.at[h, s - 1], r3.at[h, s - 1], (a, col_to(s))).wait_recv()
+    for h in range(KVH):
+        arrived(gland.at[h], r3.at[h])
         dk_acc[...] = jnp.zeros_like(dk_acc)
         dv_acc[...] = jnp.zeros_like(dv_acc)
 
@@ -288,9 +279,8 @@
         for s in SPOTS:
             to = col_to(s)
             half, rows = chunk(to)
-            copy = send(gp.at[h, half, rows, :], gland.at[s - 1, h], s4.at[h, s - 1], r4.at[h, s - 1], (a, to))
+            copy = send(gp.at[h, half, rows, :], gland.at[h, s - 1], s4, r4.at[h], (a, to))
             copy.start()
-            fourth.append(copy)
 
     transposed_tables(kvcat, kv_ref, kt, vt)
     dks[...] = jnp.zeros_like(dks)
@@ -307,12 +297,9 @@
             dks[h] += sum(p[0] for p in parts)
             dvs[h] += sum(p[1] for p in parts)
 
-    fifth = []
-    sixth = []
-
     def to_owners(p):
-        for copy in fifth[p * PAIRS * len(LANES):(p + 1) * PAIRS * len(LANES)]:
-            copy.wait_recv()
+        for u in range(PAIRS):
+            arrived(gland2[p * PAIRS + u].at[pl.ds(1, N_DP - 1)], r5.at[p * PAIRS + u])
         for s in SPOTS + [0]:
             number = inv[s]
             at = jnp.maximum(number - 1, 0)
@@ -326,24 +313,21 @@
                 else:
                     send3[p, s - 1, u] = piece
             if s:
-                copy = send(send3.at[p, s - 1], fin.at[p, s], s6.at[p, s - 1], r6.at[p, s - 1], (a, col_to(s)))
+                copy = send(send3.at[p, s - 1], fin.at[p, s], s6, r6.at[p], (a, col_to(s)))
                 copy.start()
-                sixth.append(copy)
 
     for h in range(KVH):
         finish_part(FINISH_CUTS[h], FINISH_CUTS[h + 1])
-        for copy in fourth[h * len(SPOTS):(h + 1) * len(SPOTS)]:
-            copy.wait_recv()
+        arrived(gland.at[h], r4.at[h])
         total = gp[h, my_half, my_rows, :].astype(F32)
         for s in SPOTS:
-            total += gland[s - 1, h].astype(F32)
+            total += gland[h, s - 1].astype(F32)
         total = total.astype(BF16)
         for j in range(NP):
             gmine[h, j] = total[:, j * HEAD:(j + 1) * HEAD]
         for s in LANES:
-            copy = send(gmine.at[h], gland2[h].at[s], s5.at[h, s - 1], r5.at[h, s - 1], (row_to(s), c))
+            copy = send(gmine.at[h], gland2[h].at[s], s5, r5.at[h], (row_to(s), c))
             copy.start()
-            fifth.append(copy)
         gland2[h][0] = gmine[h]
         if h == KVH - 1:
             to_owners(0)
@@ -355,24 +339,26 @@
         gr_ref[:, h * HEAD:(h + 1) * HEAD] = (dks[h] * SCALE).astype(BF16)
         gr_ref[:, HALF + h * HEAD:HALF + (h + 1) * HEAD] = dvs[h].astype(BF16)
 
-    for copy in sixth:
-        copy.wait_recv()
+    for p in range(KVH // PAIRS):
+        arrived(fin.at[p, pl.ds(1, N_RESP - 1)], r6.at[p])
     for s in range(N_RESP):
         half, rows = chunk(col_from(s))
         for h in range(KVH):
             lanes = pl.ds(pl.multiple_of(half * HALF + h * HEAD, HEAD), HEAD)
             gp_out[rows, lanes] = fin[h // PAIRS, s, h % PAIRS].astype(F32)
 
-    for copy in first + second + third + fourth + fifth + sixth:
-        copy.wait_send()
+    gone(buf1.at[pl.ds(1, N_RESP - 1)], s1)
+    gone(send2, s2)
+    gone(gland, s3)
+    gone(gland, s4)
+    gone(send2, s5)
+    gone(send3, s6)
 
 
 def local(queries, response_kv, cotangent, prompt_kv, resp_lengths, resp_prompt, owners):
     vm = pl.BlockSpec(memory_space=pltpu.VMEM)
     sm = pl.BlockSpec(memory_space=pltpu.SMEM)
     hbm = pl.BlockSpec(memory_space=pl.ANY)
-    peers = (N_RESP - 1,)
-    row_peers = (N_DP - 1,)
     dma = pltpu.SemaphoreType.DMA
     outs = pl.pallas_call(
         kernel,
@@ -410,19 +396,19 @@
             *[pltpu.VMEM((N_DP, CH, WIDE), BF16)] * KVH,
             pltpu.VMEM((KVH, CH, WIDE), BF16),
             pltpu.VMEM((KVH, 2, LP, WIDE), BF16),
-            pltpu.VMEM((N_RESP - 1, KVH, CH, WIDE), BF16),
+            pltpu.VMEM((KVH, N_RESP - 1, CH, WIDE), BF16),
             pltpu.VMEM((KVH, NP, CH, HEAD), BF16),
             *[pltpu.VMEM((N_DP, NP, CH, HEAD), BF16)] * KVH,
             pltpu.VMEM((KVH // PAIRS, N_RESP - 1, PAIRS, CH, HEAD), BF16),
             pltpu.VMEM((KVH // PAIRS, N_RESP, PAIRS, CH, HEAD), BF16),
             pltpu.SMEM((N_RESP,), jnp.int32),
             dma((3,)),
-            dma(peers), dma(peers),
-            dma((KVH,) + row_peers), dma((KVH,) + row_peers),
-            dma((KVH,) + peers), dma((KVH,) + peers),
-            dma((KVH,) + peers), dma((KVH,) + peers),
-            dma((KVH,) + row_peers), dma((KVH,) + row_peers),
-            dma((KVH // PAIRS,) + peers), dma((KVH // PAIRS,) + peers),
+            dma, dma,
+            dma, dma((KVH,)),
+            dma, dma((KVH,)),
+            dma, dma((KVH,)),
+            dma, dma((KVH,)),
+            dma, dma((KVH // PAIRS,)),
         ],
         compiler_params=pltpu.CompilerParams(
             collective_id=0, has_side_effects=True, vmem_limit_bytes=50 * 2 ** 20

time: 62.3 us -> 58.5 us (0.939)
  Pallas kernels: 57.3 us -> 53.6 us
    pallas_call x1, Pallas kernels: 57.3 us -> 53.6 us  [local(): pl.pallas_call(kernel, in_specs=[hbm, hbm, hbm, vm, sm, sm, sm], out_spec...]
where the time goes in v4:
time: 58.5 us; the launch traced here: 58.4 us
  Pallas kernels  53.6 us (92%)
  local copies, waits for them, and re-layouts  4.23 us (7%)
  between operations  0.64 us (1%)
    pallas_call x1, Pallas kernels, local(): pl.pallas_call(kernel, in_specs=[hbm, hbm, hbm, vm, sm, sm, sm], out_spec...  53.6 us
    unnamed x4, local copies, waits for them, and re-layouts  4.23 us

profile of v4, /device:TPU:1, one launch (start us, length us, event | category | flops | bytes accessed | tf_op | source)
XLA Modules:
  0.0 58.4 jit_solution(13538880380746801069)
XLA Ops:
  0.6 53.6 %grouped_attention.1 = (bf16[256,4096]{1,0:T(8,128)(2,1)S(1)}, bf16[256,4096]{1,0:T(8,128)(2,1)S(1)}, bf16[256,1024]{1,0:T(8,128)(2,1)S(1)}, f32[128,1024]{1,0:T(8,128)S(1)}) custom-call(bf16[256,4096]{1,0:T(8,128)(2,1)} %bitcast.15, bf16[256,4096]{1,0:T(8,128)(2,1)} %bitcast.16, bf16[256,1024]{1,0:T(8,128)(2,1)} %bitcast.17, bf16[128,1024]{1,0:T(8,128)(2,1)} %bitcast.18, ...), custom_call_target="tpu_custom_call" | custom-call | tf_op jit(solution)/shard_map/grouped_attention/pallas_call | solution.py:363
  54.2 1.3 %copy.15 = bf16[1,256,4096]{2,1,0:T(8,128)(2,1)} copy(bf16[1,256,4096]{2,1,0:T(8,128)(2,1)S(1)} %bitcast.12) | data formatting | bytes 4194304
  55.5 1.3 %copy.16 = bf16[1,256,4096]{2,1,0:T(8,128)(2,1)} copy(bf16[1,256,4096]{2,1,0:T(8,128)(2,1)S(1)} %bitcast.11) | data formatting | bytes 4194304
  56.8 0.8 %copy.17 = bf16[1,256,1024]{2,1,0:T(8,128)(2,1)} copy(bf16[1,256,1024]{2,1,0:T(8,128)(2,1)S(1)} %bitcast.14) | data formatting | bytes 1048576
  57.6 0.8 %copy.18 = f32[1,1,128,1024]{3,2,1,0:T(8,128)} copy(f32[1,1,128,1024]{3,2,1,0:T(8,128)S(1)} %bitcast.13) | data formatting | bytes 1048576

commit v5 on v4

--- a/solution.py
+++ b/solution.py
@@ -139,14 +139,15 @@
 
 
 def kernel(
-    q_hbm, do_hbm, kv_hbm, slot_ref, len_ref, prm_ref, own_ref,
+    q_hbm, do_hbm, kv_hbm, slot_hbm, len_ref, prm_ref, own_ref,
     out_ref, dq_ref, gr_ref, gp_out,
-    q_ref, do_ref, kv_ref,
+    q_ref, do_ref, kv_ref, slot_ref,
     bias, qmask, lmask, qt, dt, e_self, dp_self, stat, kvcat, kt, vt, w_pr, ds_pr, dk_acc, dv_acc, dks, dvs,
-    buf1, send2, got_a, got_b, got_c, got_d, mine, gp, gland, gmine, back_a, back_b, back_c, back_d, send3, fin, inv,
-    in_sem, s1, r1, s2, r2, s3, r3, s4, r4, s5, r5, s6, r6,
+    buf1, send2, pair_a, pair_b, got_a, got_b, mine, gp, gland, gmine, back_a, back_b, back_c, back_d, send3, fin, inv,
+    in_sem, s0, r0, s1, r1, s2, r2, s3, r3, s4, r4, s5, r5, s6, r6,
 ):
-    recv2 = (got_a, got_b, got_c, got_d)
+    pair = (pair_a, pair_b)
+    recv2 = (got_a, got_b)
     gland2 = (back_a, back_b, back_c, back_d)
     a = lax.axis_index("dp")
     c = lax.axis_index("resp")
@@ -155,30 +156,39 @@
 
     loads = [
         pltpu.make_async_copy(src, dst, in_sem.at[i])
-        for i, (src, dst) in enumerate(((kv_hbm, kv_ref), (q_hbm, q_ref), (do_hbm, do_ref)))
+        for i, (src, dst) in enumerate(((slot_hbm, slot_ref), (kv_hbm, kv_ref), (q_hbm, q_ref), (do_hbm, do_ref)))
     ]
     for load in loads:
         load.start()
 
+    xs = [lax.rem(x + i, 4) for i in range(4)]
+    ks = [core, 1 - core]
+    zs = [lax.rem(z + i, 4) for i in range(4)]
+    ys = [lax.rem(y + i, 4) for i in range(4)]
+    halves = [v // 2 for v in zs]
+    blocks = [(v - 2 * w) * 4 for v, w in zip(zs, halves)]
+
     def col_to(s):
-        return lax.rem(z + s // 4, 4) * 4 + lax.rem(y + s % 4, 4)
-
-    def col_from(s):
-        return lax.rem(z + 4 - s // 4, 4) * 4 + lax.rem(y + 4 - s % 4, 4)
+        return zs[s // 4] * 4 + ys[s % 4]
 
     def row_to(s):
-        return lax.rem(x + s // 2, 4) * 2 + lax.rem(core + s % 2, 2)
+        return xs[s // 2] * 2 + ks[s % 2]
 
     def spot_of(column):
-        return lax.rem(z + 4 - jnp.right_shift(column, 2), 4) * 4 + lax.rem(y + 4 - jnp.bitwise_and(column, 3), 4)
-
-    def lane_of(row):
-        return lax.rem(x + 4 - jnp.right_shift(row, 1), 4) * 2 + lax.rem(core + 2 - jnp.bitwise_and(row, 1), 2)
-
-    def chunk(index):
-        half = index // 8
-        block = lax.rem(index, 8)
-        return half, pl.ds(pl.multiple_of(block * CH, CH), CH)
+        dz = jnp.bitwise_and(z + 4 - jnp.right_shift(column, 2), 3)
+        return dz * 4 + jnp.bitwise_and(y + 4 - jnp.bitwise_and(column, 3), 3)
+
+    def lane_of(px, pk):
+        return jnp.bitwise_and(x + 4 - px, 3) * 2 + jnp.bitwise_and(core + 2 - pk, 1)
+
+    def chunk(dz, dy):
+        return halves[dz % 4], pl.ds(pl.multiple_of((blocks[dz % 4] + ys[dy % 4]) * CH, CH), CH)
+
+    def chunk_to(s):
+        return chunk(s // 4, s % 4)
+
+    def chunk_from(s):
+        return chunk(-(s // 4), -(s % 4))
 
     def send(src, dst, ssem, rsem, device):
         return pltpu.make_async_remote_copy(
@@ -198,12 +208,13 @@
         pl.semaphore_signal(barrier, inc=1, device_id=(row_to(s), c), device_id_type=MESH)
     build_masks(len_ref, prm_ref, bias, qmask, lmask)
     pl.semaphore_wait(barrier, len(SPOTS) + len(LANES))
-
-    my_half, my_rows = chunk(c)
+    loads[0].wait()
+
+    my_half, my_rows = chunk(0, 0)
 
     for s in SPOTS:
         to = col_to(s)
-        half, rows = chunk(to)
+        half, rows = chunk_to(s)
         lanes = pl.ds(pl.multiple_of(half * HALF, HALF), HALF)
         copy = send(slot_ref.at[rows, lanes], buf1.at[s], s1, r1, (a, to))
         copy.start()
@@ -217,7 +228,7 @@
             found = [jnp.maximum(found[k], found[k + 1]) for k in range(0, len(found), 2)]
         inv[s] = found[0]
 
-    for load in loads:
+    for load in loads[1:]:
         load.wait()
 
     def self_part(lo, hi):
@@ -229,32 +240,40 @@
     self_part(SELF_CUTS[0], SELF_CUTS[1])
 
     arrived(buf1.at[pl.ds(1, N_RESP - 1)], r1)
-    spots = {
-        (s, j): spot_of(jnp.bitwise_and(own_ref[j, row_to(s)], N_RESP - 1)) for s in range(N_DP) for j in range(NP)
-    }
-    for h in range(KVH):
+    for u in range(2):
+        lanes = pl.ds(pl.multiple_of((ks[1] + 2 * u) * HEAD, HEAD), HEAD)
+        send(buf1.at[:, :, lanes], pair[u].at[core], s0, r0.at[u], (row_to(1), c)).start()
+    for u in range(2):
+        pair[u][core] = buf1[:, :, pl.ds(pl.multiple_of((core + 2 * u) * HEAD, HEAD), HEAD)]
+    owned = {}
+    for s in range(N_DP):
+        for j in range(NP):
+            owner = own_ref[j, row_to(s)]
+            owned[s, j] = jnp.bitwise_and(jnp.right_shift(owner, 4), 1), spot_of(jnp.bitwise_and(owner, N_RESP - 1))
+    for u in range(2):
+        arrived(pair[u].at[0], r0.at[u])
         for s in LANES + [0]:
             for j in range(NP):
-                piece = buf1[spots[s, j], :, h * HEAD:(h + 1) * HEAD]
+                piece = pair[u][owned[s, j][0], owned[s, j][1]]
                 if s == 0:
-                    recv2[h][0, :, j * HEAD:(j + 1) * HEAD] = piece
+                    recv2[u][0, :, j * HEAD:(j + 1) * HEAD] = piece
                 else:
-                    send2[h, s - 1, :, j * HEAD:(j + 1) * HEAD] = piece
+                    send2[u, s - 1, :, j * HEAD:(j + 1) * HEAD] = piece
             if s:
-                copy = send(send2.at[h, s - 1], recv2[h].at[s], s2, r2.at[h], (row_to(s), c))
-                copy.start()
+                send(send2.at[u, s - 1], recv2[u].at[s], s2, r2.at[u], (row_to(s), c)).start()
 
     self_part(SELF_CUTS[1], SELF_CUTS[2])
 
-    from_lane = [lane_of(jnp.right_shift(own_ref[j, a], 4)) for j in range(NP)]
+    from_chip = [jnp.right_shift(own_ref[j, a], 5) for j in range(NP)]
     for h in range(KVH):
-        arrived(recv2[h].at[pl.ds(1, N_DP - 1)], r2.at[h])
+        u, k = h // 2, h % 2
+        if k == 0:
+            arrived(recv2[u].at[pl.ds(1, N_DP - 1)], r2.at[u])
         for j in range(NP):
             at = slice(j * HEAD, (j + 1) * HEAD)
-            mine[h, :, at] = recv2[h][from_lane[j], :, at]
+            mine[h, :, at] = recv2[u][lane_of(from_chip[j], k), :, at]
         for s in SPOTS:
-            copy = send(mine.at[h], kvcat.at[my_half, h, my_rows, :], s3, r3.at[h], (a, col_to(s)))
-            copy.start()
+            send(mine.at[h], kvcat.at[my_half, h, my_rows, :], s3, r3.at[h], (a, col_to(s))).start()
         kvcat[my_half, h, my_rows, :] = mine[h]
         self_part(SELF_CUTS[2 + h], SELF_CUTS[3 + h])
 
@@ -278,7 +297,7 @@
         gp[h, 1] = dv_acc[...].astype(BF16)
         for s in SPOTS:
             to = col_to(s)
-            half, rows = chunk(to)
+            half, rows = chunk_to(s)
             copy = send(gp.at[h, half, rows, :], gland.at[h, s - 1], s4, r4.at[h], (a, to))
             copy.start()
 
@@ -303,7 +322,7 @@
         for s in SPOTS + [0]:
             number = inv[s]
             at = jnp.maximum(number - 1, 0)
-            lane = lane_of(jnp.right_shift(at, 2))
+            lane = lane_of(jnp.right_shift(at, 3), jnp.bitwise_and(jnp.right_shift(at, 2), 1))
             j = jnp.bitwise_and(at, 3)
             for u in range(PAIRS):
                 piece = gland2[p * PAIRS + u][lane, j].astype(F32)
@@ -342,17 +361,27 @@
     for p in range(KVH // PAIRS):
         arrived(fin.at[p, pl.ds(1, N_RESP - 1)], r6.at[p])
     for s in range(N_RESP):
-        half, rows = chunk(col_from(s))
+        half, rows = chunk_from(s)
         for h in range(KVH):
             lanes = pl.ds(pl.multiple_of(half * HALF + h * HEAD, HEAD), HEAD)
             gp_out[rows, lanes] = fin[h // PAIRS, s, h % PAIRS].astype(F32)
 
+    gone(pair_a, s0)
     gone(buf1.at[pl.ds(1, N_RESP - 1)], s1)
     gone(send2, s2)
     gone(gland, s3)
     gone(gland, s4)
-    gone(send2, s5)
+    gone(gland.at[pl.ds(0, 2), pl.ds(0, 2 * (N_DP - 1))], s5)
     gone(send3, s6)
+
+
+def store_kernel(*refs):
+    sems = refs[8]
+    copies = [pltpu.make_async_copy(refs[i], refs[4 + i], sems.at[i]) for i in range(4)]
+    for copy in copies:
+        copy.start()
+    for copy in copies:
+        copy.wait()
 
 
 def local(queries, response_kv, cotangent, prompt_kv, resp_lengths, resp_prompt, owners):
@@ -362,7 +391,7 @@
     dma = pltpu.SemaphoreType.DMA
     outs = pl.pallas_call(
         kernel,
-        in_specs=[hbm, hbm, hbm, vm, sm, sm, sm],
+        in_specs=[hbm, hbm, hbm, hbm, sm, sm, sm],
         out_specs=[vm] * 4,
         out_shape=[
             pltpu.VMEM((TOK, 4096), BF16),
@@ -374,6 +403,7 @@
             pltpu.VMEM((TOK, 4096), BF16),
             pltpu.VMEM((TOK, 4096), BF16),
             pltpu.VMEM((TOK, 1024), BF16),
+            pltpu.VMEM((LP, 1024), BF16),
             pltpu.VMEM((TOK, TOK), F32),
             pltpu.VMEM((NP, TOK, HEAD), BF16),
             pltpu.VMEM((NP, LP, TOK), BF16),
@@ -392,8 +422,9 @@
             pltpu.VMEM((KVH, TOK, HEAD), F32),
             pltpu.VMEM((KVH, TOK, HEAD), F32),
             pltpu.VMEM((N_RESP, CH, HALF), BF16),
-            pltpu.VMEM((KVH, N_DP - 1, CH, WIDE), BF16),
-            *[pltpu.VMEM((N_DP, CH, WIDE), BF16)] * KVH,
+            pltpu.VMEM((2, N_DP - 1, CH, WIDE), BF16),
+            *[pltpu.VMEM((2, N_RESP, CH, HEAD), BF16)] * 2,
+            *[pltpu.VMEM((N_DP, CH, WIDE), BF16)] * 2,
             pltpu.VMEM((KVH, CH, WIDE), BF16),
             pltpu.VMEM((KVH, 2, LP, WIDE), BF16),
             pltpu.VMEM((KVH, N_RESP - 1, CH, WIDE), BF16),
@@ -402,23 +433,37 @@
             pltpu.VMEM((KVH // PAIRS, N_RESP - 1, PAIRS, CH, HEAD), BF16),
             pltpu.VMEM((KVH // PAIRS, N_RESP, PAIRS, CH, HEAD), BF16),
             pltpu.SMEM((N_RESP,), jnp.int32),
-            dma((3,)),
+            dma((4,)),
+            dma, dma((2,)),
             dma, dma,
-            dma, dma((KVH,)),
+            dma, dma((2,)),
             dma, dma((KVH,)),
             dma, dma((KVH,)),
             dma, dma((KVH,)),
             dma, dma((KVH // PAIRS,)),
         ],
         compiler_params=pltpu.CompilerParams(
-            collective_id=0, has_side_effects=True, vmem_limit_bytes=50 * 2 ** 20
+            collective_id=0, has_side_effects=True, vmem_limit_bytes=58 * 2 ** 20
         ),
         name="grouped_attention",
     )(
         queries[0], cotangent[0], response_kv[0], prompt_kv[0, 0],
         resp_lengths[0], resp_prompt[0], owners.T,
     )
-    attn_out, grad_queries, grad_response, grad_prompt = outs
+    attn_out, grad_queries, grad_response, grad_prompt = pl.pallas_call(
+        store_kernel,
+        in_specs=[vm] * 4,
+        out_specs=[hbm] * 4,
+        out_shape=[
+            jax.ShapeDtypeStruct((TOK, 4096), BF16),
+            jax.ShapeDtypeStruct((TOK, 4096), BF16),
+            jax.ShapeDtypeStruct((TOK, 1024), BF16),
+            jax.ShapeDtypeStruct((LP, 1024), F32),
+        ],
+        scratch_shapes=[dma((4,))],
+        compiler_params=pltpu.CompilerParams(vmem_limit_bytes=2 ** 20),
+        name="store_outputs",
+    )(*[pltpu.with_memory_space_constraint(out, pltpu.VMEM) for out in outs])
     return attn_out[None], grad_queries[None], grad_response[None], grad_prompt[None, None]
 
 

time: 58.5 us -> 56.4 us (0.964)
  local copies, waits for them, and re-layouts: 4.23 us -> 0 us
  Pallas kernels: 53.6 us -> 55.4 us
    unnamed x4 -> x0, local copies, waits for them, and re-layouts: 4.23 us -> none
    pallas_call x1 -> x2, Pallas kernels: 53.6 us -> 55.4 us  [the longest x1 53.1 us: local(): pl.pallas_call(kernel, in_specs=[hbm, hbm, hbm, hbm, sm, sm, sm], out_spe...]
where the time goes in v5:
time: 56.4 us; the launch traced here: 56.2 us
  Pallas kernels  55.4 us (98%)
  between operations  0.8 us (1%)
    pallas_call x1, Pallas kernels, local(): pl.pallas_call(kernel, in_specs=[hbm, hbm, hbm, hbm, sm, sm, sm], out_spe...  53.1 us
    pallas_call x1, Pallas kernels, local(): pl.pallas_call(store_kernel, in_specs=[vm] * 4, out_specs=[hbm] * 4, out_...  2.37 us

profile of v5, /device:TPU:1, one launch (start us, length us, event | category | flops | bytes accessed | tf_op | source)
XLA Modules:
  0.0 56.2 jit_solution(17958776885313475604)
XLA Ops:
  0.6 53.1 %grouped_attention.1 = (bf16[256,4096]{1,0:T(8,128)(2,1)S(1)}, bf16[256,4096]{1,0:T(8,128)(2,1)S(1)}, bf16[256,1024]{1,0:T(8,128)(2,1)S(1)}, f32[128,1024]{1,0:T(8,128)S(1)}) custom-call(bf16[256,4096]{1,0:T(8,128)(2,1)} %bitcast.11, bf16[256,4096]{1,0:T(8,128)(2,1)} %bitcast.12, bf16[256,1024]{1,0:T(8,128)(2,1)} %bitcast.13, bf16[128,1024]{1,0:T(8,128)(2,1)} %bitcast.14, ...), custom_call_target="tpu_custom_call" | custom-call | tf_op jit(solution)/shard_map/grouped_attention/pallas_call | solution.py:392
  53.7 2.4 %store_outputs.1 = (bf16[256,4096]{1,0:T(8,128)(2,1)}, bf16[256,4096]{1,0:T(8,128)(2,1)}, bf16[256,1024]{1,0:T(8,128)(2,1)}, f32[128,1024]{1,0:T(8,128)}) custom-call(bf16[256,4096]{1,0:T(8,128)(2,1)S(1)} %get-tuple-element.12.refs_0_, bf16[256,4096]{1,0:T(8,128)(2,1)S(1)} %get-tuple-element.13.refs_1_, bf16[256,1024]{1,0:T(8,128)(2,1)S(1)} %get-tuple-element.14.refs_2_, ...), custom_call_target="tpu_custom_call" | custom-call | tf_op jit(solution)/shard_map/store_outputs/pallas_call | solution.py:453

commit v6 on v5

--- a/solution.py
+++ b/solution.py
@@ -135,6 +135,7 @@
 PAIRS = 2
 MESH = pl.DeviceIdType.MESH
 SPOTS = sorted(range(1, N_RESP), key=lambda s: -(min(s // 4, 4 - s // 4) + min(s % 4, 4 - s % 4)))
+MIXED = (10, 9, 6, 11, 14, 5, 15, 7, 13, 8, 2, 4, 1, 12, 3)
 LANES = sorted(range(1, N_DP), key=lambda s: -min(s // 2, 4 - s // 2))
 
 
@@ -272,7 +273,7 @@
         for j in range(NP):
             at = slice(j * HEAD, (j + 1) * HEAD)
             mine[h, :, at] = recv2[u][lane_of(from_chip[j], k), :, at]
-        for s in SPOTS:
+        for s in MIXED:
             send(mine.at[h], kvcat.at[my_half, h, my_rows, :], s3, r3.at[h], (a, col_to(s))).start()
         kvcat[my_half, h, my_rows, :] = mine[h]
         self_part(SELF_CUTS[2 + h], SELF_CUTS[3 + h])
@@ -295,7 +296,7 @@
 
         gp[h, 0] = (dk_acc[...] * SCALE).astype(BF16)
         gp[h, 1] = dv_acc[...].astype(BF16)
-        for s in SPOTS:
+        for s in MIXED:
             to = col_to(s)
             half, rows = chunk_to(s)
             copy = send(gp.at[h, half, rows, :], gland.at[h, s - 1], s4, r4.at[h], (a, to))
@@ -337,6 +338,8 @@
 
     for h in range(KVH):
         finish_part(FINISH_CUTS[h], FINISH_CUTS[h + 1])
+        if h == KVH - 1:
+            to_owners(0)
         arrived(gland.at[h], r4.at[h])
         total = gp[h, my_half, my_rows, :].astype(F32)
         for s in SPOTS:
@@ -348,8 +351,6 @@
             copy = send(gmine.at[h], gland2[h].at[s], s5, r5.at[h], (row_to(s), c))
             copy.start()
         gland2[h][0] = gmine[h]
-        if h == KVH - 1:
-            to_owners(0)
     finish_part(FINISH_CUTS[4], FINISH_CUTS[5])
     to_owners(1)
     finish_part(FINISH_CUTS[5], FINISH_CUTS[6])

time: 56.4 us -> 58.5 us (1.037)
  Pallas kernels: 55.4 us -> 57.6 us
    pallas_call x1, Pallas kernels: 53.1 us -> 55.2 us  [local(): pl.pallas_call(kernel, in_specs=[hbm, hbm, hbm, hbm, sm, sm, sm], out_spe...]
where the time goes in v6:
time: 58.5 us; the launch traced here: 58.4 us
  Pallas kernels  57.6 us (98%)
  between operations  0.8 us (1%)
    pallas_call x1, Pallas kernels, local(): pl.pallas_call(kernel, in_specs=[hbm, hbm, hbm, hbm, sm, sm, sm], out_spe...  55.2 us
    pallas_call x1, Pallas kernels, local(): pl.pallas_call(store_kernel, in_specs=[vm] * 4, out_specs=[hbm] * 4, out_...  2.37 us

profile of v6, /device:TPU:1, one launch (start us, length us, event | category | flops | bytes accessed | tf_op | source)
XLA Modules:
  0.0 58.4 jit_solution(11864177934452137798)
XLA Ops:
  0.6 55.2 %grouped_attention.1 = (bf16[256,4096]{1,0:T(8,128)(2,1)S(1)}, bf16[256,4096]{1,0:T(8,128)(2,1)S(1)}, bf16[256,1024]{1,0:T(8,128)(2,1)S(1)}, f32[128,1024]{1,0:T(8,128)S(1)}) custom-call(bf16[256,4096]{1,0:T(8,128)(2,1)} %bitcast.11, bf16[256,4096]{1,0:T(8,128)(2,1)} %bitcast.12, bf16[256,1024]{1,0:T(8,128)(2,1)} %bitcast.13, bf16[128,1024]{1,0:T(8,128)(2,1)} %bitcast.14, ...), custom_call_target="tpu_custom_call" | custom-call | tf_op jit(solution)/shard_map/grouped_attention/pallas_call | solution.py:393
  55.9 2.4 %store_outputs.1 = (bf16[256,4096]{1,0:T(8,128)(2,1)}, bf16[256,4096]{1,0:T(8,128)(2,1)}, bf16[256,1024]{1,0:T(8,128)(2,1)}, f32[128,1024]{1,0:T(8,128)}) custom-call(bf16[256,4096]{1,0:T(8,128)(2,1)S(1)} %get-tuple-element.12.refs_0_, bf16[256,4096]{1,0:T(8,128)(2,1)S(1)} %get-tuple-element.13.refs_1_, bf16[256,1024]{1,0:T(8,128)(2,1)S(1)} %get-tuple-element.14.refs_2_, ...), custom_call_target="tpu_custom_call" | custom-call | tf_op jit(solution)/shard_map/store_outputs/pallas_call | solution.py:454
